TPU v7x, 512 devices: a whole 4x4x16 slice. The times are simulated.
512 devices in a mesh: sec: 8 (over z_hi, core), tile: 64 (over z_lo, x, y).
Axes of the slice: x: 4, y: 4, z: 16 (z_hi: 4, z_lo: 4; z = z_hi * 4 + z_lo), core: 2. Of those that a mesh axis runs over, the one named last changes fastest.
Arguments:
- displacement: float32 [8, 2, 128, 4096], P('sec', None, 'tile'), may hold values from -6 to 6
- stiffness: float32 [8, 128, 4096], P('sec', 'tile'), may hold values from 0.5 to 2
- match_weight: float32 [8, 192, 512], P('sec', 'tile'), may hold values from 0.5 to 4
- match_offset: float32 [8, 2, 192, 512], P('sec', None, 'tile'), may hold values from -6 to 6
- source_row: int32 [8, 192, 512], P('sec', 'tile'), may hold values from 0 to 1
- source_col: int32 [8, 192, 512], P('sec', 'tile'), may hold values from 0 to 4095
- target_row: int32 [8, 192, 512], P('sec', 'tile'), may hold values from 0 to 1
- target_col: int32 [8, 192, 512], P('sec', 'tile'), may hold values from 0 to 4095
- match_count: int32 [8, 192], P('sec', 'tile'), may hold values from 0 to 512, as said below
Outputs:
- aligned: float32 [8, 2, 128, 4096], P('sec', None, 'tile')
Inputs may be any that keep to these rules, and one draw needn't show every extreme that they name: `match_count`: in every section some tile's group 1 uses all 512 slots, and some tile other than the first and the last uses all 512 slots in group 0 and in group 2.
All inputs are finite; a program needn't handle non-finite values.
Results may differ from a plain program's by a relative error of at most 0.0018.
Values sent between devices are 32-bit elements; how exact they have to be, the bound alone decides.
No kernel may reach another device: no remote copies, remote signals or barrier semaphores. Data moves between devices by JAX's collectives and lax.ppermute only.
A program may use at most 64 MiB of HBM per device.

v0:
```python
import jax
import jax.numpy as jnp
from jax import lax
from jax.sharding import PartitionSpec as P

STEPS = 2


neighbours = [
    (-1, 0, 1.0),
    (1, 0, 1.0),
    (0, -1, 1.0),
    (0, 1, 1.0),
    (-1, -1, 0.5),
    (-1, 1, 0.5),
    (1, -1, 0.5),
    (1, 1, 0.5),
]
damping = 0.7


def passed_along(value, axis, steps):
    count = lax.axis_size(axis)
    initial, last = (max(0, -steps), min(count, count - steps))
    return lax.ppermute(value, axis, [(source, source + steps) for source in range(initial, last)])


def padded_2(cells, sides, width):
    for axis, dim in sides:
        count = lax.axis_size(axis)
        ends = count - 1
        head = lax.slice_in_dim(cells, 0, width, axis=dim)
        tail = lax.slice_in_dim(cells, cells.shape[dim] - width, cells.shape[dim], axis=dim)
        cells = jnp.concatenate(
            [
                lax.ppermute(tail, axis, [(i, (i + 1) % count) for i in range(ends)]),
                cells,
                lax.ppermute(head, axis, [((i + 1) % count, i) for i in range(ends)]),
            ],
            axis=dim,
        )
    return cells


def springs(padded_u, padded_c, field, stiff_now):
    row_count = field.shape[1]
    col_count = field.shape[2]
    force = jnp.zeros_like(field)
    total = jnp.zeros_like(stiff_now)
    for row_shift, col_shift, factor in neighbours:
        near_u = padded_u[
            :, 1 + row_shift : 1 + row_shift + row_count, 1 + col_shift : 1 + col_shift + col_count
        ]
        near_c = padded_c[
            1 + row_shift : 1 + row_shift + row_count, 1 + col_shift : 1 + col_shift + col_count
        ]
        spring = factor * stiff_now * near_c
        force = force + spring[None] * (near_u - field)
        total = total + spring
    return (force, total)


def split_parts(values):
    high = values.astype(jnp.bfloat16)
    rest = values - high.astype(jnp.float32)
    middle = rest.astype(jnp.bfloat16)
    low = (rest - middle.astype(jnp.float32)).astype(jnp.bfloat16)
    return jnp.concatenate([high, middle, low], axis=0)


def block_size(slot_total, node_total):
    return min(slot_total, max(8, (1 << 22) // node_total))


def gather_slots(values, node_ids):
    width = values.shape[0]
    node_total = values.shape[1]
    slot_total = node_ids.shape[0]
    size = block_size(slot_total, node_total)
    parts = split_parts(values)
    node_range = jnp.arange(node_total, dtype=jnp.int32)

    def gather_one_block(carry, ids_block):
        hot_block = (ids_block[:, None] == node_range[None, :]).astype(jnp.bfloat16)
        picked = lax.dot_general(
            parts, hot_block, (((1,), (1,)), ((), ())), preferred_element_type=jnp.float32
        )
        picked = picked.reshape(3, width, size)
        return (carry, picked[0] + picked[1] + picked[2])

    unused, blocks = lax.scan(
        gather_one_block, jnp.float32(0.0), node_ids.reshape(slot_total // size, size)
    )
    return blocks.transpose(1, 0, 2).reshape(width, slot_total)


def spread_slots(values, node_ids, node_total):
    width = values.shape[0]
    slot_total = node_ids.shape[0]
    size = block_size(slot_total, node_total)
    count_blocks = slot_total // size
    parts = split_parts(values).reshape(3 * width, count_blocks, size).transpose(1, 0, 2)
    node_range = jnp.arange(node_total, dtype=jnp.int32)

    def spread_one_block(carry, pieces):
        ids_block, part_block = pieces
        hot_block = (ids_block[:, None] == node_range[None, :]).astype(jnp.bfloat16)
        summed = jnp.dot(part_block, hot_block, preferred_element_type=jnp.float32).reshape(
            3, width, node_total
        )
        return (carry + (summed[0] + summed[1] + summed[2]), None)

    start = jnp.zeros((width, node_total), jnp.float32)
    result, unused = lax.scan(
        spread_one_block, start, (node_ids.reshape(count_blocks, size), parts)
    )
    return result


def to_next(payload):
    return passed_along(payload, "sec", 1)


def across(payload):
    widened = padded_2(payload, (("tile", 0),), 1)
    return widened[0::2]


def back_across(payload):
    widened = padded_2(payload, (("tile", 0),), 1)
    return widened[0::2]


def to_prev(payload):
    return passed_along(payload, "sec", -1)


def body(
    displacement,
    stiffness,
    match_weight,
    match_offset,
    source_row,
    source_col,
    target_row,
    target_col,
    match_count,
):
    field = displacement[0]
    stiff_now = stiffness[0]
    row_count = field.shape[1]
    col_count = field.shape[2]
    node_total = row_count * col_count
    slots = match_weight.shape[2]
    sec_index = lax.axis_index("sec")
    tile_index = lax.axis_index("tile")
    n_sec = lax.axis_size("sec")
    n_tile = lax.axis_size("tile")
    groups = jnp.arange(3, dtype=jnp.int32)
    dest_tile = tile_index + groups - 1
    slot_ids = jnp.arange(slots, dtype=jnp.int32)
    usable = (slot_ids[None, :] < match_count[0][:, None]) & (sec_index < n_sec - 1)
    usable = usable & ((dest_tile >= 0) & (dest_tile < n_tile))[:, None]
    weight = jnp.where(usable, match_weight[0], jnp.float32(0.0))
    source_idx = (source_row[0] * col_count + source_col[0]).reshape(-1)
    target_idx = (target_row[0] * col_count + target_col[0]).reshape(-1)
    offset = match_offset[0]
    saved_c = stiff_now
    for sweep_no in range(STEPS):
        stacked = jnp.concatenate([field, stiff_now[None]], axis=0)
        padded = padded_2(stacked, (("tile", 1),), 1)
        saved_c = padded[2]
        padded_u = jnp.pad(padded[:2], ((0, 0), (0, 0), (1, 1)))
        padded_c = jnp.pad(saved_c, ((0, 0), (1, 1)))
        force, total = springs(padded_u, padded_c, field, stiff_now)
        flat_u = field.reshape(2, node_total)
        source_vals = gather_slots(flat_u, source_idx).reshape(2, 3, slots) - offset
        payload = jnp.stack([source_vals[0], source_vals[1], weight], axis=1)
        arrived = across(to_next(payload))
        arrived_weight = arrived[:, 2]
        target_vals = gather_slots(flat_u, target_idx).reshape(2, 3, slots)
        pull = arrived_weight[None] * (target_vals - arrived[:, 0:2].transpose(1, 0, 2))
        answer = pull.transpose(1, 0, 2)
        returned = to_prev(back_across(answer))
        target_terms = jnp.concatenate(
            [-pull.reshape(2, -1), arrived_weight.reshape(1, -1)], axis=0
        )
        source_terms = jnp.concatenate(
            [returned.transpose(1, 0, 2).reshape(2, -1), weight.reshape(1, -1)], axis=0
        )
        at_target = spread_slots(target_terms, target_idx, node_total)
        at_source = spread_slots(source_terms, source_idx, node_total)
        flat_force = force.reshape(2, node_total) + at_target[:2] + at_source[:2]
        flat_total = total.reshape(-1) + at_target[2] + at_source[2]
        field = field + damping * (flat_force / flat_total[None]).reshape(2, row_count, col_count)
    return field[None]


def solution(mesh):
    placed = (
        P("sec", None, "tile", None),
        P("sec", "tile", None),
        P("sec", "tile", None),
        P("sec", None, "tile", None),
        P("sec", "tile", None),
        P("sec", "tile", None),
        P("sec", "tile", None),
        P("sec", "tile", None),
        P("sec", "tile"),
    )
    return jax.shard_map(
        body, mesh=mesh, in_specs=placed, out_specs=P("sec", None, "tile", None), check_vma=False
    )
```

profile of v0, /device:TPU:415, one launch (start us, length us, event | category | flops | bytes accessed | tf_op | source)
XLA Modules:
  0.0 166.1 jit_solution(5282740731352516984)
XLA Ops:
  1.9 8.9 %while.88 = (s32[]{:T(128)}, f32[3,2,512]{2,1,0:T(2,128)S(1)}, s32[3,512]{1,0:T(4,128)S(1)}, bf16[6,8192]{1,0:T(8,128)(2,1)S(1)}, s32[]{:T(128)}) while((s32[]{:T(128)}, f32[3,2,512]{2,1,0:T(2,128)S(1)}, s32[3,512]{1,0:T(4,128)S(1)}, bf16[6,8192]{1,0:T(8,128)(2,1)S(1)}, s32[]{:T(128)}) %tuple.177), condition=%wide.region_1.2_spmd.clone, body=%wide.region_0.1_spmd.clone.sunk | while | flops 54528000 | bytes 133197 | solution.py:91
  2.0 2.9 %fusion.157 = f32[6,512]{1,0:T(8,128)S(1)} fusion(bf16[6,8192]{1,0:T(8,128)(2,1)S(1)} %get-tuple-element.689, s32[512]{0:T(512)S(1)} %bitcast.247), kind=kOutput, calls=%fused_computation.11.clone.1 | convolution fusion | flops 54525952 | bytes 112640 | tf_op jit(solution)/shard_map/while/body/eval_jaxpr/dot_general | solution.py:85
  4.9 2.9 %fusion.157 = f32[6,512]{1,0:T(8,128)S(1)} fusion(bf16[6,8192]{1,0:T(8,128)(2,1)S(1)} %get-tuple-element.689, s32[512]{0:T(512)S(1)} %bitcast.247), kind=kOutput, calls=%fused_computation.11.clone.1 | convolution fusion | flops 54525952 | bytes 112640 | tf_op jit(solution)/shard_map/while/body/eval_jaxpr/dot_general | solution.py:85
  7.9 2.9 %fusion.157 = f32[6,512]{1,0:T(8,128)S(1)} fusion(bf16[6,8192]{1,0:T(8,128)(2,1)S(1)} %get-tuple-element.689, s32[512]{0:T(512)S(1)} %bitcast.247), kind=kOutput, calls=%fused_computation.11.clone.1 | convolution fusion | flops 54525952 | bytes 112640 | tf_op jit(solution)/shard_map/while/body/eval_jaxpr/dot_general | solution.py:85
  12.4 2.4 %collective-permute-start.1 = (f32[3,1,4096]{2,1,0:T(1,128)S(1)}, f32[3,1,4096]{2,1,0:T(1,128)S(1)}, u32[]{:S(2)}, u32[]{:S(2)}) collective-permute-start(f32[3,1,4096]{2,1,0:T(1,128)S(1)} %get-tuple-element.433), channel_id=1, source_target_pairs={{1,0},{2,1},{3,2},{4,3},{5,4},{6,5},{7,6},{8,7},{9,8},{10,9},{11,1... | collective-permute-start | bytes 147464 | tf_op jit(solution)/shard_map/ppermute | solution.py:38
  14.8 7.1 %collective-permute-start = (f32[3,1,4096]{2,1,0:T(1,128)S(1)}, f32[3,1,4096]{2,1,0:T(1,128)S(1)}, u32[]{:S(2)}, u32[]{:S(2)}) collective-permute-start(f32[3,1,4096]{2,1,0:T(1,128)S(1)} %get-tuple-element.434), channel_id=1, source_target_pairs={{0,1},{1,2},{2,3},{3,4},{4,5},{5,6},{6,7},{7,8},{8,9},{9,10},{10,1... | collective-permute-start | bytes 147464 | tf_op jit(solution)/shard_map/ppermute | solution.py:36
  22.0 8.9 %while.89 = (s32[]{:T(128)}, f32[3,2,512]{2,1,0:T(2,128)S(1)}, s32[3,512]{1,0:T(4,128)S(1)}, bf16[6,8192]{1,0:T(8,128)(2,1)S(1)}, s32[]{:T(128)}) while((s32[]{:T(128)}, f32[3,2,512]{2,1,0:T(2,128)S(1)}, s32[3,512]{1,0:T(4,128)S(1)}, bf16[6,8192]{1,0:T(8,128)(2,1)S(1)}, s32[]{:T(128)}) %tuple.204), condition=%wide.region_3.4_spmd.clone, body=%wide.region_2.3_spmd.clone.sunk | while | flops 54528000 | bytes 133197 | solution.py:91
  22.0 2.9 %fusion.160 = f32[6,512]{1,0:T(8,128)S(1)} fusion(bf16[6,8192]{1,0:T(8,128)(2,1)S(1)} %get-tuple-element.674, s32[512]{0:T(512)S(1)} %bitcast.248), kind=kOutput, calls=%fused_computation.20.clone.1 | convolution fusion | flops 54525952 | bytes 112640 | tf_op jit(solution)/shard_map/while/body/eval_jaxpr/dot_general | solution.py:85
  24.9 2.9 %fusion.160 = f32[6,512]{1,0:T(8,128)S(1)} fusion(bf16[6,8192]{1,0:T(8,128)(2,1)S(1)} %get-tuple-element.674, s32[512]{0:T(512)S(1)} %bitcast.248), kind=kOutput, calls=%fused_computation.20.clone.1 | convolution fusion | flops 54525952 | bytes 112640 | tf_op jit(solution)/shard_map/while/body/eval_jaxpr/dot_general | solution.py:85
  27.9 2.9 %fusion.160 = f32[6,512]{1,0:T(8,128)S(1)} fusion(bf16[6,8192]{1,0:T(8,128)(2,1)S(1)} %get-tuple-element.674, s32[512]{0:T(512)S(1)} %bitcast.248), kind=kOutput, calls=%fused_computation.20.clone.1 | convolution fusion | flops 54525952 | bytes 112640 | tf_op jit(solution)/shard_map/while/body/eval_jaxpr/dot_general | solution.py:85
  30.8 1.9 %collective-permute-start.3 = (f32[1,3,512]{2,1,0:T(4,128)S(1)}, f32[1,3,512]{2,1,0:T(4,128)S(1)}, u32[]{:S(2)}, u32[]{:S(2)}) collective-permute-start(f32[1,3,512]{2,1,0:T(4,128)S(1)} %get-tuple-element.443), channel_id=1, source_target_pairs={{0,1},{1,2},{2,3},{3,4},{4,5},{5,6},{6,7},{7,8},{8,9},{9,10},{10,1... | collective-permute-start | bytes 18440 | tf_op jit(solution)/shard_map/ppermute | solution.py:36
  32.8 3.4 %collective-permute-start.4 = (f32[1,3,512]{2,1,0:T(4,128)S(1)}, f32[1,3,512]{2,1,0:T(4,128)S(1)}, u32[]{:S(2)}, u32[]{:S(2)}) collective-permute-start(f32[1,3,512]{2,1,0:T(4,128)S(1)} %get-tuple-element.444), channel_id=1, source_target_pairs={{1,0},{2,1},{3,2},{4,3},{5,4},{6,5},{7,6},{8,7},{9,8},{10,9},{11,1... | collective-permute-start | bytes 18440 | tf_op jit(solution)/shard_map/ppermute | solution.py:38
  36.3 5.1 %collective-permute-done.4 = f32[1,3,512]{2,1,0:T(4,128)S(1)} collective-permute-done((f32[1,3,512]{2,1,0:T(4,128)S(1)}, f32[1,3,512]{2,1,0:T(4,128)S(1)}, u32[]{:S(2)}, u32[]{:S(2)}) %collective-permute-start.4) | collective-permute-done | bytes 6176 | tf_op jit(solution)/shard_map/ppermute | solution.py:38
  41.5 1.9 %collective-permute-start.5 = (f32[1,2,512]{2,1,0:T(2,128)S(1)}, f32[1,2,512]{2,1,0:T(2,128)S(1)}, u32[]{:S(2)}, u32[]{:S(2)}) collective-permute-start(f32[1,2,512]{2,1,0:T(2,128)S(1)} %get-tuple-element.457), channel_id=1, source_target_pairs={{0,1},{1,2},{2,3},{3,4},{4,5},{5,6},{6,7},{7,8},{8,9},{9,10},{10,1... | collective-permute-start | bytes 12296 | tf_op jit(solution)/shard_map/ppermute | solution.py:36
  43.5 3.4 %collective-permute-start.6 = (f32[1,2,512]{2,1,0:T(2,128)S(1)}, f32[1,2,512]{2,1,0:T(2,128)S(1)}, u32[]{:S(2)}, u32[]{:S(2)}) collective-permute-start(f32[1,2,512]{2,1,0:T(2,128)S(1)} %get-tuple-element.458), channel_id=1, source_target_pairs={{1,0},{2,1},{3,2},{4,3},{5,4},{6,5},{7,6},{8,7},{9,8},{10,9},{11,1... | collective-permute-start | bytes 12296 | tf_op jit(solution)/shard_map/ppermute | solution.py:38
  46.9 5.1 %collective-permute-done.6 = f32[1,2,512]{2,1,0:T(2,128)S(1)} collective-permute-done((f32[1,2,512]{2,1,0:T(2,128)S(1)}, f32[1,2,512]{2,1,0:T(2,128)S(1)}, u32[]{:S(2)}, u32[]{:S(2)}) %collective-permute-start.6) | collective-permute-done | bytes 4128 | tf_op jit(solution)/shard_map/ppermute | solution.py:38
  52.1 6.2 %collective-permute-start.7 = (f32[3,2,512]{2,1,0:T(2,128)S(1)}, f32[3,2,512]{2,1,0:T(2,128)S(1)}, u32[]{:S(2)}, u32[]{:S(2)}) collective-permute-start(f32[3,2,512]{2,1,0:T(2,128)S(1)} %slice.368), channel_id=1, source_target_pairs={{64,0},{128,64},{192,128},{256,192},{320,256},{384,320},{448,384},... | collective-permute-start | bytes 36872 | tf_op jit(solution)/shard_map/ppermute | solution.py:25
  58.3 9.9 %while.92 = (s32[]{:T(128)}, f32[3,8192]{1,0:T(4,128)S(1)}, bf16[3,9,512]{2,1,0:T(8,128)(2,1)S(1)}, s32[3,512]{1,0:T(4,128)S(1)}, s32[]{:T(128)}, /*index=5*/s32[]{:T(128)}) while((s32[]{:T(128)}, f32[3,8192]{1,0:T(4,128)S(1)}, bf16[3,9,512]{2,1,0:T(8,128)(2,1)S(1)}, s32[3,512]{1,0:T(4,128)S(1)}, s32[]{:T(128)}, ...), condition=%wide.region_5.6_spmd.clone, body=%wide.region_4.5_spmd.clone.sunk | while | flops 79790080 | bytes 809055 | solution.py:114
  58.3 3.1 %fusion.169 = f32[9,8192]{1,0:T(8,128)S(1)} fusion(s32[512]{0:T(512)S(1)} %bitcast.243, bf16[3,9,512]{2,1,0:T(8,128)(2,1)S(1)} %get-tuple-element.723, s32[]{:T(128)S(6)} %copy.61), kind=kOutput, calls=%fused_computation.45.clone.1 | convolution fusion | flops 79691776 | bytes 313348 | tf_op jit(solution)/shard_map/while/body/eval_jaxpr/dot_general | solution.py:108
  61.7 3.1 %fusion.169 = f32[9,8192]{1,0:T(8,128)S(1)} fusion(s32[512]{0:T(512)S(1)} %bitcast.243, bf16[3,9,512]{2,1,0:T(8,128)(2,1)S(1)} %get-tuple-element.723, s32[]{:T(128)S(6)} %copy.61), kind=kOutput, calls=%fused_computation.45.clone.1 | convolution fusion | flops 79691776 | bytes 313348 | tf_op jit(solution)/shard_map/while/body/eval_jaxpr/dot_general | solution.py:108
  65.0 3.1 %fusion.169 = f32[9,8192]{1,0:T(8,128)S(1)} fusion(s32[512]{0:T(512)S(1)} %bitcast.243, bf16[3,9,512]{2,1,0:T(8,128)(2,1)S(1)} %get-tuple-element.723, s32[]{:T(128)S(6)} %copy.61), kind=kOutput, calls=%fused_computation.45.clone.1 | convolution fusion | flops 79691776 | bytes 313348 | tf_op jit(solution)/shard_map/while/body/eval_jaxpr/dot_general | solution.py:108
  68.4 9.9 %while.93 = (s32[]{:T(128)}, f32[3,8192]{1,0:T(4,128)S(1)}, bf16[3,9,512]{2,1,0:T(8,128)(2,1)S(1)}, s32[3,512]{1,0:T(4,128)S(1)}, s32[]{:T(128)}, /*index=5*/s32[]{:T(128)}) while((s32[]{:T(128)}, f32[3,8192]{1,0:T(4,128)S(1)}, bf16[3,9,512]{2,1,0:T(8,128)(2,1)S(1)}, s32[3,512]{1,0:T(4,128)S(1)}, s32[]{:T(128)}, ...), condition=%wide.region_7.8_spmd.clone, body=%wide.region_6.7_spmd.clone.sunk | while | flops 79790080 | bytes 809055 | solution.py:114
  68.4 3.1 %fusion.172 = f32[9,8192]{1,0:T(8,128)S(1)} fusion(s32[512]{0:T(512)S(1)} %bitcast.244, bf16[3,9,512]{2,1,0:T(8,128)(2,1)S(1)} %get-tuple-element.705, s32[]{:T(128)S(6)} %copy.55), kind=kOutput, calls=%fused_computation.55.clone.1 | convolution fusion | flops 79691776 | bytes 313348 | tf_op jit(solution)/shard_map/while/body/eval_jaxpr/dot_general | solution.py:108
  71.7 3.1 %fusion.172 = f32[9,8192]{1,0:T(8,128)S(1)} fusion(s32[512]{0:T(512)S(1)} %bitcast.244, bf16[3,9,512]{2,1,0:T(8,128)(2,1)S(1)} %get-tuple-element.705, s32[]{:T(128)S(6)} %copy.55), kind=kOutput, calls=%fused_computation.55.clone.1 | convolution fusion | flops 79691776 | bytes 313348 | tf_op jit(solution)/shard_map/while/body/eval_jaxpr/dot_general | solution.py:108
  75.0 3.1 %fusion.172 = f32[9,8192]{1,0:T(8,128)S(1)} fusion(s32[512]{0:T(512)S(1)} %bitcast.244, bf16[3,9,512]{2,1,0:T(8,128)(2,1)S(1)} %get-tuple-element.705, s32[]{:T(128)S(6)} %copy.55), kind=kOutput, calls=%fused_computation.55.clone.1 | convolution fusion | flops 79691776 | bytes 313348 | tf_op jit(solution)/shard_map/while/body/eval_jaxpr/dot_general | solution.py:108
  80.0 8.9 %while.90 = (s32[]{:T(128)}, f32[3,2,512]{2,1,0:T(2,128)S(1)}, s32[3,512]{1,0:T(4,128)S(1)}, bf16[6,8192]{1,0:T(8,128)(2,1)S(1)}, s32[]{:T(128)}) while((s32[]{:T(128)}, f32[3,2,512]{2,1,0:T(2,128)S(1)}, s32[3,512]{1,0:T(4,128)S(1)}, bf16[6,8192]{1,0:T(8,128)(2,1)S(1)}, s32[]{:T(128)}) %tuple.199), condition=%wide.region_9.10_spmd.clone, body=%wide.region_8.9_spmd.clone.sunk | while | flops 54528000 | bytes 133197 | solution.py:91
  80.0 2.9 %fusion.163 = f32[6,512]{1,0:T(8,128)S(1)} fusion(bf16[6,8192]{1,0:T(8,128)(2,1)S(1)} %get-tuple-element.755, s32[512]{0:T(512)S(1)} %bitcast.249), kind=kOutput, calls=%fused_computation.29.clone.1 | convolution fusion | flops 54525952 | bytes 112640 | tf_op jit(solution)/shard_map/while/body/eval_jaxpr/dot_general | solution.py:85
  83.0 2.9 %fusion.163 = f32[6,512]{1,0:T(8,128)S(1)} fusion(bf16[6,8192]{1,0:T(8,128)(2,1)S(1)} %get-tuple-element.755, s32[512]{0:T(512)S(1)} %bitcast.249), kind=kOutput, calls=%fused_computation.29.clone.1 | convolution fusion | flops 54525952 | bytes 112640 | tf_op jit(solution)/shard_map/while/body/eval_jaxpr/dot_general | solution.py:85
  85.9 2.9 %fusion.163 = f32[6,512]{1,0:T(8,128)S(1)} fusion(bf16[6,8192]{1,0:T(8,128)(2,1)S(1)} %get-tuple-element.755, s32[512]{0:T(512)S(1)} %bitcast.249), kind=kOutput, calls=%fused_computation.29.clone.1 | convolution fusion | flops 54525952 | bytes 112640 | tf_op jit(solution)/shard_map/while/body/eval_jaxpr/dot_general | solution.py:85
  88.9 9.1 %while.91 = (s32[]{:T(128)}, f32[3,2,512]{2,1,0:T(2,128)S(1)}, s32[3,512]{1,0:T(4,128)S(1)}, bf16[6,8192]{1,0:T(8,128)(2,1)S(1)}, s32[]{:T(128)}) while((s32[]{:T(128)}, f32[3,2,512]{2,1,0:T(2,128)S(1)}, s32[3,512]{1,0:T(4,128)S(1)}, bf16[6,8192]{1,0:T(8,128)(2,1)S(1)}, s32[]{:T(128)}) %tuple.205), condition=%wide.region_11.12_spmd.clone, body=%wide.region_10.11_spmd.clone.sunk | while | flops 54528000 | bytes 133197 | solution.py:91
  89.1 2.9 %fusion.166 = f32[6,512]{1,0:T(8,128)S(1)} fusion(bf16[6,8192]{1,0:T(8,128)(2,1)S(1)} %get-tuple-element.740, s32[512]{0:T(512)S(1)} %bitcast.250), kind=kOutput, calls=%fused_computation.38.clone.1 | convolution fusion | flops 54525952 | bytes 112640 | tf_op jit(solution)/shard_map/while/body/eval_jaxpr/dot_general | solution.py:85
  92.1 2.9 %fusion.166 = f32[6,512]{1,0:T(8,128)S(1)} fusion(bf16[6,8192]{1,0:T(8,128)(2,1)S(1)} %get-tuple-element.740, s32[512]{0:T(512)S(1)} %bitcast.250), kind=kOutput, calls=%fused_computation.38.clone.1 | convolution fusion | flops 54525952 | bytes 112640 | tf_op jit(solution)/shard_map/while/body/eval_jaxpr/dot_general | solution.py:85
  95.1 2.9 %fusion.166 = f32[6,512]{1,0:T(8,128)S(1)} fusion(bf16[6,8192]{1,0:T(8,128)(2,1)S(1)} %get-tuple-element.740, s32[512]{0:T(512)S(1)} %bitcast.250), kind=kOutput, calls=%fused_computation.38.clone.1 | convolution fusion | flops 54525952 | bytes 112640 | tf_op jit(solution)/shard_map/while/body/eval_jaxpr/dot_general | solution.py:85
  99.4 4.0 %collective-permute-done.10 = f32[3,3,512]{2,1,0:T(4,128)S(1)} collective-permute-done((f32[3,3,512]{2,1,0:T(4,128)S(1)}, f32[3,3,512]{2,1,0:T(4,128)S(1)}, u32[]{:S(2)}, u32[]{:S(2)}) %collective-permute-start.10) | collective-permute-done | bytes 18464 | tf_op jit(solution)/shard_map/ppermute | solution.py:25
  105.3 3.4 %collective-permute-start.12 = (f32[1,3,512]{2,1,0:T(4,128)S(1)}, f32[1,3,512]{2,1,0:T(4,128)S(1)}, u32[]{:S(2)}, u32[]{:S(2)}) collective-permute-start(f32[1,3,512]{2,1,0:T(4,128)S(1)} %get-tuple-element.440), channel_id=1, source_target_pairs={{1,0},{2,1},{3,2},{4,3},{5,4},{6,5},{7,6},{8,7},{9,8},{10,9},{11,1... | collective-permute-start | bytes 18440 | tf_op jit(solution)/shard_map/ppermute | solution.py:38
  108.9 6.1 %collective-permute-start.8 = (f32[3,1,4096]{2,1,0:T(1,128)S(1)}, f32[3,1,4096]{2,1,0:T(1,128)S(1)}, u32[]{:S(2)}, u32[]{:S(2)}) collective-permute-start(f32[3,1,4096]{2,1,0:T(1,128)S(1)} %get-tuple-element.429), channel_id=1, source_target_pairs={{0,1},{1,2},{2,3},{3,4},{4,5},{5,6},{6,7},{7,8},{8,9},{9,10},{10,1... | collective-permute-start | bytes 147464 | tf_op jit(solution)/shard_map/ppermute | solution.py:36
  117.1 7.6 %collective-permute-start.13 = (f32[1,2,512]{2,1,0:T(2,128)S(1)}, f32[1,2,512]{2,1,0:T(2,128)S(1)}, u32[]{:S(2)}, u32[]{:S(2)}) collective-permute-start(f32[1,2,512]{2,1,0:T(2,128)S(1)} %get-tuple-element.453), channel_id=1, source_target_pairs={{0,1},{1,2},{2,3},{3,4},{4,5},{5,6},{6,7},{7,8},{8,9},{9,10},{10,1... | collective-permute-start | bytes 12296 | tf_op jit(solution)/shard_map/ppermute | solution.py:36
  124.7 1.9 %collective-permute-start.14 = (f32[1,2,512]{2,1,0:T(2,128)S(1)}, f32[1,2,512]{2,1,0:T(2,128)S(1)}, u32[]{:S(2)}, u32[]{:S(2)}) collective-permute-start(f32[1,2,512]{2,1,0:T(2,128)S(1)} %get-tuple-element.454), channel_id=1, source_target_pairs={{1,0},{2,1},{3,2},{4,3},{5,4},{6,5},{7,6},{8,7},{9,8},{10,9},{11,1... | collective-permute-start | bytes 12296 | tf_op jit(solution)/shard_map/ppermute | solution.py:38
  126.7 6.6 %collective-permute-done.14 = f32[1,2,512]{2,1,0:T(2,128)S(1)} collective-permute-done((f32[1,2,512]{2,1,0:T(2,128)S(1)}, f32[1,2,512]{2,1,0:T(2,128)S(1)}, u32[]{:S(2)}, u32[]{:S(2)}) %collective-permute-start.14) | collective-permute-done | bytes 4128 | tf_op jit(solution)/shard_map/ppermute | solution.py:38
  133.3 10.7 %collective-permute-start.15 = (f32[3,2,512]{2,1,0:T(2,128)S(1)}, f32[3,2,512]{2,1,0:T(2,128)S(1)}, u32[]{:S(2)}, u32[]{:S(2)}) collective-permute-start(f32[3,2,512]{2,1,0:T(2,128)S(1)} %slice.404), channel_id=1, source_target_pairs={{64,0},{128,64},{192,128},{256,192},{320,256},{384,320},{448,384},... | collective-permute-start | bytes 36872 | tf_op jit(solution)/shard_map/ppermute | solution.py:25
  144.0 9.9 %while.94 = (s32[]{:T(128)}, f32[3,8192]{1,0:T(4,128)S(1)}, bf16[3,9,512]{2,1,0:T(8,128)(2,1)S(1)}, s32[3,512]{1,0:T(4,128)S(1)}, s32[]{:T(128)}, /*index=5*/s32[]{:T(128)}) while((s32[]{:T(128)}, f32[3,8192]{1,0:T(4,128)S(1)}, bf16[3,9,512]{2,1,0:T(8,128)(2,1)S(1)}, s32[3,512]{1,0:T(4,128)S(1)}, s32[]{:T(128)}, ...), condition=%wide.region_13.14_spmd.clone, body=%wide.region_12.13_spmd.clone.sunk | while | flops 79790080 | bytes 809055 | solution.py:114
  144.0 3.1 %fusion.175 = f32[9,8192]{1,0:T(8,128)S(1)} fusion(s32[512]{0:T(512)S(1)} %bitcast.245, bf16[3,9,512]{2,1,0:T(8,128)(2,1)S(1)} %get-tuple-element.789, s32[]{:T(128)S(6)} %copy.85), kind=kOutput, calls=%fused_computation.65.clone.1 | convolution fusion | flops 79691776 | bytes 313348 | tf_op jit(solution)/shard_map/while/body/eval_jaxpr/dot_general | solution.py:108
  147.3 3.1 %fusion.175 = f32[9,8192]{1,0:T(8,128)S(1)} fusion(s32[512]{0:T(512)S(1)} %bitcast.245, bf16[3,9,512]{2,1,0:T(8,128)(2,1)S(1)} %get-tuple-element.789, s32[]{:T(128)S(6)} %copy.85), kind=kOutput, calls=%fused_computation.65.clone.1 | convolution fusion | flops 79691776 | bytes 313348 | tf_op jit(solution)/shard_map/while/body/eval_jaxpr/dot_general | solution.py:108
  150.6 3.1 %fusion.175 = f32[9,8192]{1,0:T(8,128)S(1)} fusion(s32[512]{0:T(512)S(1)} %bitcast.245, bf16[3,9,512]{2,1,0:T(8,128)(2,1)S(1)} %get-tuple-element.789, s32[]{:T(128)S(6)} %copy.85), kind=kOutput, calls=%fused_computation.65.clone.1 | convolution fusion | flops 79691776 | bytes 313348 | tf_op jit(solution)/shard_map/while/body/eval_jaxpr/dot_general | solution.py:108
  154.0 9.9 %while.95 = (s32[]{:T(128)}, f32[3,8192]{1,0:T(4,128)S(1)}, bf16[3,9,512]{2,1,0:T(8,128)(2,1)S(1)}, s32[3,512]{1,0:T(4,128)S(1)}, s32[]{:T(128)}, /*index=5*/s32[]{:T(128)}) while((s32[]{:T(128)}, f32[3,8192]{1,0:T(4,128)S(1)}, bf16[3,9,512]{2,1,0:T(8,128)(2,1)S(1)}, s32[3,512]{1,0:T(4,128)S(1)}, s32[]{:T(128)}, ...), condition=%wide.region_15.16_spmd.clone, body=%wide.region_14.15_spmd.clone.sunk | while | flops 79790080 | bytes 809055 | solution.py:114
  154.0 3.1 %fusion.178 = f32[9,8192]{1,0:T(8,128)S(1)} fusion(s32[512]{0:T(512)S(1)} %bitcast.246, bf16[3,9,512]{2,1,0:T(8,128)(2,1)S(1)} %get-tuple-element.771, s32[]{:T(128)S(6)} %copy.79), kind=kOutput, calls=%fused_computation.75.clone.1 | convolution fusion | flops 79691776 | bytes 313348 | tf_op jit(solution)/shard_map/while/body/eval_jaxpr/dot_general | solution.py:108
  157.3 3.1 %fusion.178 = f32[9,8192]{1,0:T(8,128)S(1)} fusion(s32[512]{0:T(512)S(1)} %bitcast.246, bf16[3,9,512]{2,1,0:T(8,128)(2,1)S(1)} %get-tuple-element.771, s32[]{:T(128)S(6)} %copy.79), kind=kOutput, calls=%fused_computation.75.clone.1 | convolution fusion | flops 79691776 | bytes 313348 | tf_op jit(solution)/shard_map/while/body/eval_jaxpr/dot_general | solution.py:108
  160.6 3.1 %fusion.178 = f32[9,8192]{1,0:T(8,128)S(1)} fusion(s32[512]{0:T(512)S(1)} %bitcast.246, bf16[3,9,512]{2,1,0:T(8,128)(2,1)S(1)} %get-tuple-element.771, s32[]{:T(128)S(6)} %copy.79), kind=kOutput, calls=%fused_computation.75.clone.1 | convolution fusion | flops 79691776 | bytes 313348 | tf_op jit(solution)/shard_map/while/body/eval_jaxpr/dot_general | solution.py:108
  (160 shorter events, 14.9 us)
Async XLA Ops:
  1.8 9.0 %copy-start.2 = (f32[1,2,3,512]{3,1,2,0:T(2,128)S(1)}, f32[1,2,3,512]{3,1,2,0:T(2,128)}, u32[]{:S(2)}) copy-start(f32[1,2,3,512]{3,1,2,0:T(2,128)} %param.28) | copy-start | bytes 36868
  1.9 9.0 %copy-start.3 = (f32[1,3,512]{2,0,1:T(1,128)S(1)}, f32[1,3,512]{2,0,1:T(1,128)}, u32[]{:S(2)}) copy-start(f32[1,3,512]{2,0,1:T(1,128)} %param.27) | copy-start | bytes 18436
  1.9 9.0 %copy-start.6 = (s32[1,3]{1,0:T(1,128)S(1)}, s32[1,3]{1,0:T(1,128)}, u32[]{:S(2)}) copy-start(s32[1,3]{1,0:T(1,128)} %param.33) | copy-start | bytes 40
  1.9 10.4 %copy-start = (f32[1,2,2,4096]{3,2,1,0:T(2,128)S(1)}, f32[1,2,2,4096]{3,2,1,0:T(2,128)}, u32[]{:S(2)}) copy-start(f32[1,2,2,4096]{3,2,1,0:T(2,128)} %param.25) | copy-start | bytes 196612
  1.9 10.4 %copy-start.1 = (f32[1,2,4096]{2,1,0:T(2,128)S(1)}, f32[1,2,4096]{2,1,0:T(2,128)}, u32[]{:S(2)}) copy-start(f32[1,2,4096]{2,1,0:T(2,128)} %param.26) | copy-start | bytes 98308
  1.9 20.0 %copy-start.4 = (s32[1,3,512]{2,0,1:T(1,128)S(1)}, s32[1,3,512]{2,0,1:T(1,128)}, u32[]{:S(2)}) copy-start(s32[1,3,512]{2,0,1:T(1,128)} %param.32) | copy-start | bytes 18436
  1.9 20.0 %copy-start.5 = (s32[1,3,512]{2,0,1:T(1,128)S(1)}, s32[1,3,512]{2,0,1:T(1,128)}, u32[]{:S(2)}) copy-start(s32[1,3,512]{2,0,1:T(1,128)} %param.31) | copy-start | bytes 18436
  11.0 19.8 %collective-permute-start.2 = (f32[3,3,512]{2,1,0:T(4,128)S(1)}, f32[3,3,512]{2,1,0:T(4,128)S(1)}, u32[]{:S(2)}, u32[]{:S(2)}) collective-permute-start(f32[3,3,512]{2,1,0:T(4,128)S(1)} %pad_maximum_fusion.13), channel_id=1, source_target_pairs={{0,64},{64,128},{128,192},{192,256},{256,320},{320,384},{384,448},... | collective-permute-start | bytes 55304 | tf_op jit(solution)/shard_map/ppermute | solution.py:25
  12.4 65.9 %collective-permute-start.1 = (f32[3,1,4096]{2,1,0:T(1,128)S(1)}, f32[3,1,4096]{2,1,0:T(1,128)S(1)}, u32[]{:S(2)}, u32[]{:S(2)}) collective-permute-start(f32[3,1,4096]{2,1,0:T(1,128)S(1)} %get-tuple-element.433), channel_id=1, source_target_pairs={{1,0},{2,1},{3,2},{4,3},{5,4},{6,5},{7,6},{8,7},{9,8},{10,9},{11,1... | collective-permute-start | bytes 147464 | tf_op jit(solution)/shard_map/ppermute | solution.py:38
  14.8 63.5 %collective-permute-start = (f32[3,1,4096]{2,1,0:T(1,128)S(1)}, f32[3,1,4096]{2,1,0:T(1,128)S(1)}, u32[]{:S(2)}, u32[]{:S(2)}) collective-permute-start(f32[3,1,4096]{2,1,0:T(1,128)S(1)} %get-tuple-element.434), channel_id=1, source_target_pairs={{0,1},{1,2},{2,3},{3,4},{4,5},{5,6},{6,7},{7,8},{8,9},{9,10},{10,1... | collective-permute-start | bytes 147464 | tf_op jit(solution)/shard_map/ppermute | solution.py:36
  30.8 5.4 %collective-permute-start.3 = (f32[1,3,512]{2,1,0:T(4,128)S(1)}, f32[1,3,512]{2,1,0:T(4,128)S(1)}, u32[]{:S(2)}, u32[]{:S(2)}) collective-permute-start(f32[1,3,512]{2,1,0:T(4,128)S(1)} %get-tuple-element.443), channel_id=1, source_target_pairs={{0,1},{1,2},{2,3},{3,4},{4,5},{5,6},{6,7},{7,8},{8,9},{9,10},{10,1... | collective-permute-start | bytes 18440 | tf_op jit(solution)/shard_map/ppermute | solution.py:36
  32.8 8.6 %collective-permute-start.4 = (f32[1,3,512]{2,1,0:T(4,128)S(1)}, f32[1,3,512]{2,1,0:T(4,128)S(1)}, u32[]{:S(2)}, u32[]{:S(2)}) collective-permute-start(f32[1,3,512]{2,1,0:T(4,128)S(1)} %get-tuple-element.444), channel_id=1, source_target_pairs={{1,0},{2,1},{3,2},{4,3},{5,4},{6,5},{7,6},{8,7},{9,8},{10,9},{11,1... | collective-permute-start | bytes 18440 | tf_op jit(solution)/shard_map/ppermute | solution.py:38
  41.5 5.3 %collective-permute-start.5 = (f32[1,2,512]{2,1,0:T(2,128)S(1)}, f32[1,2,512]{2,1,0:T(2,128)S(1)}, u32[]{:S(2)}, u32[]{:S(2)}) collective-permute-start(f32[1,2,512]{2,1,0:T(2,128)S(1)} %get-tuple-element.457), channel_id=1, source_target_pairs={{0,1},{1,2},{2,3},{3,4},{4,5},{5,6},{6,7},{7,8},{8,9},{9,10},{10,1... | collective-permute-start | bytes 12296 | tf_op jit(solution)/shard_map/ppermute | solution.py:36
  43.5 8.6 %collective-permute-start.6 = (f32[1,2,512]{2,1,0:T(2,128)S(1)}, f32[1,2,512]{2,1,0:T(2,128)S(1)}, u32[]{:S(2)}, u32[]{:S(2)}) collective-permute-start(f32[1,2,512]{2,1,0:T(2,128)S(1)} %get-tuple-element.458), channel_id=1, source_target_pairs={{1,0},{2,1},{3,2},{4,3},{5,4},{6,5},{7,6},{8,7},{9,8},{10,9},{11,1... | collective-permute-start | bytes 12296 | tf_op jit(solution)/shard_map/ppermute | solution.py:38
  52.1 16.2 %collective-permute-start.7 = (f32[3,2,512]{2,1,0:T(2,128)S(1)}, f32[3,2,512]{2,1,0:T(2,128)S(1)}, u32[]{:S(2)}, u32[]{:S(2)}) collective-permute-start(f32[3,2,512]{2,1,0:T(2,128)S(1)} %slice.368), channel_id=1, source_target_pairs={{64,0},{128,64},{192,128},{256,192},{320,256},{384,320},{448,384},... | collective-permute-start | bytes 36872 | tf_op jit(solution)/shard_map/ppermute | solution.py:25
  98.0 5.4 %collective-permute-start.10 = (f32[3,3,512]{2,1,0:T(4,128)S(1)}, f32[3,3,512]{2,1,0:T(4,128)S(1)}, u32[]{:S(2)}, u32[]{:S(2)}) collective-permute-start(f32[3,3,512]{2,1,0:T(4,128)S(1)} %pad_maximum_fusion.12), channel_id=1, source_target_pairs={{0,64},{64,128},{128,192},{192,256},{256,320},{320,384},{384,448},... | collective-permute-start | bytes 55304 | tf_op jit(solution)/shard_map/ppermute | solution.py:25
  103.4 13.5 %collective-permute-start.11 = (f32[1,3,512]{2,1,0:T(4,128)S(1)}, f32[1,3,512]{2,1,0:T(4,128)S(1)}, u32[]{:S(2)}, u32[]{:S(2)}) collective-permute-start(f32[1,3,512]{2,1,0:T(4,128)S(1)} %get-tuple-element.439), channel_id=1, source_target_pairs={{0,1},{1,2},{2,3},{3,4},{4,5},{5,6},{6,7},{7,8},{8,9},{9,10},{10,1... | collective-permute-start | bytes 18440 | tf_op jit(solution)/shard_map/ppermute | solution.py:36
  105.3 11.6 %collective-permute-start.12 = (f32[1,3,512]{2,1,0:T(4,128)S(1)}, f32[1,3,512]{2,1,0:T(4,128)S(1)}, u32[]{:S(2)}, u32[]{:S(2)}) collective-permute-start(f32[1,3,512]{2,1,0:T(4,128)S(1)} %get-tuple-element.440), channel_id=1, source_target_pairs={{1,0},{2,1},{3,2},{4,3},{5,4},{6,5},{7,6},{8,7},{9,8},{10,9},{11,1... | collective-permute-start | bytes 18440 | tf_op jit(solution)/shard_map/ppermute | solution.py:38
  108.9 55.1 %collective-permute-start.8 = (f32[3,1,4096]{2,1,0:T(1,128)S(1)}, f32[3,1,4096]{2,1,0:T(1,128)S(1)}, u32[]{:S(2)}, u32[]{:S(2)}) collective-permute-start(f32[3,1,4096]{2,1,0:T(1,128)S(1)} %get-tuple-element.429), channel_id=1, source_target_pairs={{0,1},{1,2},{2,3},{3,4},{4,5},{5,6},{6,7},{7,8},{8,9},{9,10},{10,1... | collective-permute-start | bytes 147464 | tf_op jit(solution)/shard_map/ppermute | solution.py:36
  115.0 48.9 %collective-permute-start.9 = (f32[3,1,4096]{2,1,0:T(1,128)S(1)}, f32[3,1,4096]{2,1,0:T(1,128)S(1)}, u32[]{:S(2)}, u32[]{:S(2)}) collective-permute-start(f32[3,1,4096]{2,1,0:T(1,128)S(1)} %get-tuple-element.430), channel_id=1, source_target_pairs={{1,0},{2,1},{3,2},{4,3},{5,4},{6,5},{7,6},{8,7},{9,8},{10,9},{11,1... | collective-permute-start | bytes 147464 | tf_op jit(solution)/shard_map/ppermute | solution.py:38
  117.1 9.6 %collective-permute-start.13 = (f32[1,2,512]{2,1,0:T(2,128)S(1)}, f32[1,2,512]{2,1,0:T(2,128)S(1)}, u32[]{:S(2)}, u32[]{:S(2)}) collective-permute-start(f32[1,2,512]{2,1,0:T(2,128)S(1)} %get-tuple-element.453), channel_id=1, source_target_pairs={{0,1},{1,2},{2,3},{3,4},{4,5},{5,6},{6,7},{7,8},{8,9},{9,10},{10,1... | collective-permute-start | bytes 12296 | tf_op jit(solution)/shard_map/ppermute | solution.py:36
  124.7 8.6 %collective-permute-start.14 = (f32[1,2,512]{2,1,0:T(2,128)S(1)}, f32[1,2,512]{2,1,0:T(2,128)S(1)}, u32[]{:S(2)}, u32[]{:S(2)}) collective-permute-start(f32[1,2,512]{2,1,0:T(2,128)S(1)} %get-tuple-element.454), channel_id=1, source_target_pairs={{1,0},{2,1},{3,2},{4,3},{5,4},{6,5},{7,6},{8,7},{9,8},{10,9},{11,1... | collective-permute-start | bytes 12296 | tf_op jit(solution)/shard_map/ppermute | solution.py:38
  133.3 20.6 %collective-permute-start.15 = (f32[3,2,512]{2,1,0:T(2,128)S(1)}, f32[3,2,512]{2,1,0:T(2,128)S(1)}, u32[]{:S(2)}, u32[]{:S(2)}) collective-permute-start(f32[3,2,512]{2,1,0:T(2,128)S(1)} %slice.404), channel_id=1, source_target_pairs={{64,0},{128,64},{192,128},{256,192},{320,256},{384,320},{448,384},... | collective-permute-start | bytes 36872 | tf_op jit(solution)/shard_map/ppermute | solution.py:25
where the time goes:
time: 167 us; the launch traced here: 166 us
  matrix products  72.6 us (43%)
  starting transfers between devices  62.4 us (37%)
  waiting for transfers between devices  20.9 us (13%)
  other arithmetic  6.79 us (4%)
  local copies, waits for them, and re-layouts  1.68 us (1%)
    dot_general x12, matrix products, spread_one_block(): jnp.dot(part_block, hot_block, preferred_element_type=jnp.float32)  37.7 us
    dot_general x12, matrix products, gather_one_block(): lax.dot_general(parts, hot_block, (((1,), (1,)), ((), ())), preferred_ele...  34.9 us
    ppermute x6, starting transfers between devices, padded_2(): lax.ppermute(tail, axis, [(i, (i + 1) % count) for i in range(ends)])  26.6 us
    ppermute x4, starting transfers between devices, passed_along(): lax.ppermute(value, axis, [(source, source + steps) for source in range(i...  19.5 us
    ppermute x6, waiting for transfers between devices, padded_2(): lax.ppermute(head, axis, [((i + 1) % count, i) for i in range(ends)])  16.9 us
    ppermute x6, starting transfers between devices, padded_2(): lax.ppermute(head, axis, [((i + 1) % count, i) for i in range(ends)])  16.3 us
    ppermute x4, waiting for transfers between devices, passed_along(): lax.ppermute(value, axis, [(source, source + steps) for source in range(i...  4.05 us
  transfers between devices with their start and end apart: 16, of which 4 were waited for; matrix products, arithmetic and copies ran while one was open for 30% of the time, Pallas kernels for 0%

commit v1 on v0

v1 whole, which is shorter than its diff:
```python
import jax
import jax.numpy as jnp
from jax import lax
from jax.experimental import pallas as pl
from jax.experimental.pallas import tpu as pltpu
from jax.sharding import PartitionSpec as P

damping = 0.7
LANES = 128
F32 = jnp.float32
BF16 = jnp.bfloat16
VMEM = pl.BlockSpec(memory_space=pltpu.VMEM)
SMEM = pl.BlockSpec(memory_space=pltpu.SMEM)


def halves(value):
    high = value.astype(BF16)
    return high, (value - high.astype(F32)).astype(BF16)


def one_hot(index, depth):
    place = lax.broadcasted_iota(jnp.int32, (depth, index.shape[1]), 0)
    return place == index


def gather(table, lane_hot, block_mask):
    blocks = block_mask.shape[0]
    picked = jnp.dot(table, jnp.concatenate([lane_hot, lane_hot], axis=0), preferred_element_type=F32)
    return [
        jnp.sum(jnp.where(block_mask, picked[i * blocks : (i + 1) * blocks], 0.0), axis=0, keepdims=True)
        for i in range(picked.shape[0] // blocks)
    ]


def table_of(fields):
    high, low = halves(jnp.concatenate(fields, axis=0))
    return jnp.concatenate([high, low], axis=1)


def scatter(values, lane_hot, block_hot):
    parts = [halves(v) for v in values]
    left = jnp.concatenate([block_hot * p[k] for k in range(2) for p in parts], axis=0)
    return lax.dot_general(left, lane_hot, (((1,), (1,)), ((), ())), preferred_element_type=F32)


def wide(block):
    return jnp.concatenate([block[8 * i : 8 * i + 8] for i in range(4)], axis=1)


def narrow(rows):
    return jnp.concatenate([rows[:, LANES * i : LANES * (i + 1)] for i in range(4)], axis=0)


def side_sum(block):
    count = block.shape[0]
    lane = lax.broadcasted_iota(jnp.int32, block.shape, 1)
    row = lax.broadcasted_iota(jnp.int32, block.shape, 0)
    before = pltpu.roll(block, 1, 1)
    carried = jnp.where(row == 0, 0.0, pltpu.roll(before, 1, 0))
    before = jnp.where(lane == 0, carried, before)
    after = pltpu.roll(block, LANES - 1, 1)
    carried = jnp.where(row == count - 1, 0.0, pltpu.roll(after, count - 1, 0))
    after = jnp.where(lane == LANES - 1, carried, after)
    return before + after


def stencil(above, first, second, below):
    sides = [side_sum(b) for b in (above, first, second, below)]
    upper = first + 0.5 * sides[1]
    lower = second + 0.5 * sides[2]
    return jnp.concatenate(
        [
            above + 0.5 * sides[0] + lower + sides[1],
            upper + below + 0.5 * sides[3] + sides[2],
        ],
        axis=0,
    )


def rows_of(ref, lead=()):
    return [ref[lead + (pl.ds(r, 32, 2), slice(None))] for r in range(2)]


def fill(ref, rows):
    pad = (-len(rows)) % 8
    ref[...] = jnp.concatenate(rows + [jnp.zeros_like(rows[0])] * pad, axis=0)


def send_tiles(odd_tile, left, right, even_ref, odd_ref):
    even_ref[...] = jnp.where(odd_tile, left, right)
    odd_ref[...] = jnp.where(odd_tile, right, left)


def tile_message(halo, slot_rows):
    pad = (-len(slot_rows)) % 8
    rows = [wide(h) for h in halo] + slot_rows + [jnp.zeros_like(slot_rows[0])] * pad
    return jnp.concatenate(rows, axis=0)


def first_kernel(place, count, u, c, w, off, srow, scol, trow, tcol, even_msg, odd_msg, own, ids, uo, co):
    sec, tile, n_sec, n_tile = place[0], place[1], place[2], place[3]
    field = [jnp.concatenate(rows_of(u, (i,)), axis=0) for i in range(2)]
    stiff = jnp.concatenate(rows_of(c), axis=0)
    for i in range(2):
        uo[i] = field[i]
    co[...] = stiff
    table = table_of(field)
    slot = lax.broadcasted_iota(jnp.int32, (1, w.shape[1]), 1)
    sources, targets, blocks, lanes = [], [], [], []
    for g in range(3):
        dest = tile + g - 1
        limit = jnp.where((sec < n_sec - 1) & (dest >= 0) & (dest < n_tile), count[0, g], 0)
        weight = jnp.where(slot < limit, w[g : g + 1], 0.0)
        col = scol[g : g + 1]
        block, lane = srow[g : g + 1] * 32 + (col >> 7), col & 127
        blocks.append(block)
        lanes.append(lane)
        got = gather(table, one_hot(lane, LANES).astype(BF16), one_hot(block, 64))
        sources.append([weight * (got[i] - off[i, g : g + 1]) for i in range(2)] + [weight])
    for k in range(3):
        col = tcol[k : k + 1]
        block, lane = trow[k : k + 1] * 32 + (col >> 7), col & 127
        blocks.append(block)
        lanes.append(lane)
        targets.append(gather(table, one_hot(lane, LANES).astype(BF16), one_hot(block, 64)))
    halo = [stiff * field[0], stiff * field[1], stiff]
    left = tile_message([h[:32] for h in halo], sources[0] + targets[0])
    right = tile_message([h[32:] for h in halo], sources[2] + targets[2])
    send_tiles((tile & 1) == 1, left, right, even_msg, odd_msg)
    fill(own, sources[1] + targets[1] + [s[2] for s in sources])
    fill(ids, blocks + lanes)


def both_sides(place, even_in, odd_in, rows):
    odd_tile = (place[1] & 1) == 1
    mate = 1 - (place[1] & 1)
    even = even_in[mate, rows, :]
    odd = odd_in[rows, :]
    return jnp.where(odd_tile, even, odd), jnp.where(odd_tile, odd, even)


def pack_kernel(first, place, even_in, odd_in, own, even_msg, odd_msg):
    base = 24 if first else 16
    n_src = 3 if first else 2
    left, right = both_sides(place, even_in, odd_in, slice(base, base + 8))
    own_rows = own[...]
    source = [m[i : i + 1] for m in (left, own_rows, right) for i in range(n_src)]
    target = [m[n_src + i : n_src + i + 1] for m in (left, own_rows, right) for i in range(2)]
    size = even_msg.shape[0]
    zero = jnp.zeros_like(source[0])
    source = jnp.concatenate(source + [zero] * (size - len(source)), axis=0)
    target = jnp.concatenate(target + [zero] * (size - len(target)), axis=0)
    send_tiles((place[0] & 1) == 1, target, source, even_msg, odd_msg)


def spring_kernel(first, place, even_in, odd_in, u, c, *refs):
    stiff = c[...]
    up, down = both_sides(place, even_in, odd_in, slice(0, 24 if first else 16))
    if first:
        near_ref, total_ref = refs
        fields = [stiff * u[0], stiff * u[1], stiff]
    else:
        (near_ref,) = refs
        fields = [stiff * u[0], stiff * u[1]]
    for i, f in enumerate(fields):
        near = stiff * stencil(narrow(up[8 * i : 8 * i + 8]), f[:32], f[32:], narrow(down[8 * i : 8 * i + 8]))
        if i < 2:
            near_ref[i] = near
        else:
            total_ref[...] = near


def arrivals(place, even_in, odd_in):
    odd_sec = (place[0] & 1) == 1
    mate = 1 - (place[0] & 1)
    even = even_in[mate]
    odd = odd_in[...]
    return jnp.where(odd_sec, even, odd), jnp.where(odd_sec, odd, even)


def hot_of(ids, g):
    return one_hot(ids[6 + g : 7 + g], LANES), one_hot(ids[g : g + 1], 64)


def middle_kernel(place, even_in, odd_in, own, ids, off, u, c, near, total, u_out, total_out, even_msg, odd_msg, own_out):
    source_in, target_in = arrivals(place, even_in, odd_in)
    ids = ids[...]
    acc = jnp.zeros((384, LANES), F32)
    hots = []
    weights = []
    for g in range(3):
        weight = own[5 + g : 6 + g, :]
        weights.append(weight)
        vals = [weight * (target_in[2 * g + i : 2 * g + i + 1] + off[i, g : g + 1]) for i in range(2)] + [weight]
        lane_hot, block_mask = hot_of(ids, g)
        lane_hot = lane_hot.astype(BF16)
        hots.append((lane_hot, block_mask))
        acc = acc + scatter(vals, lane_hot, block_mask.astype(BF16))
    for k in range(3):
        vals = [source_in[3 * k + i : 3 * k + i + 1] for i in range(3)]
        lane_hot, block_mask = hot_of(ids, 3 + k)
        lane_hot = lane_hot.astype(BF16)
        hots.append((lane_hot, block_mask))
        acc = acc + scatter(vals, lane_hot, block_mask.astype(BF16))
    acc = acc[:192] + acc[192:]
    share = damping / (total[...] + acc[128:192])
    total_out[...] = share
    stiff = c[...]
    field = [(1.0 - damping) * u[i] + (near[i] + acc[64 * i : 64 * i + 64]) * share for i in range(2)]
    for i in range(2):
        u_out[i] = field[i]
    table = table_of(field)
    got = [gather(table, *h) for h in hots]
    sources = [[weights[g] * (got[g][i] - off[i, g : g + 1]) for i in range(2)] for g in range(3)]
    targets = got[3:]
    halo = [stiff * field[0], stiff * field[1]]
    left = tile_message([h[:32] for h in halo], sources[0] + targets[0])
    right = tile_message([h[32:] for h in halo], sources[2] + targets[2])
    send_tiles((place[1] & 1) == 1, left, right, even_msg, odd_msg)
    fill(own_out, sources[1] + targets[1])


def last_kernel(place, even_in, odd_in, own, ids, off, u, near, share, out):
    source_in, target_in = arrivals(place, even_in, odd_in)
    ids = ids[...]
    acc = jnp.zeros((256, LANES), F32)
    for g in range(6):
        if g < 3:
            weight = own[5 + g : 6 + g, :]
            vals = [weight * (target_in[2 * g + i : 2 * g + i + 1] + off[i, g : g + 1]) for i in range(2)]
        else:
            vals = [source_in[2 * (g - 3) + i : 2 * (g - 3) + i + 1] for i in range(2)]
        lane_hot, block_mask = hot_of(ids, g)
        acc = acc + scatter(vals, lane_hot.astype(BF16), block_mask.astype(BF16))
    acc = acc[:128] + acc[128:]
    for i in range(2):
        new = (1.0 - damping) * u[i] + (near[i] + acc[64 * i : 64 * i + 64]) * share[...]
        for r in range(2):
            out[i, pl.ds(r, 32, 2), :] = new[32 * r : 32 * r + 32]


def call(kernel, shapes, *args, scalars=1):
    return pl.pallas_call(
        kernel,
        out_shape=[jax.ShapeDtypeStruct(s, d) for s, d in shapes],
        in_specs=[SMEM] * scalars + [VMEM] * (len(args) - scalars),
        out_specs=[VMEM] * len(shapes),
        compiler_params=pltpu.CompilerParams(vmem_limit_bytes=32 * 1024 * 1024),
    )(*args)


def body(n_sec, n_tile, displacement, stiffness, match_weight, match_offset, source_row, source_col, target_row, target_col, match_count):
    axes = ("sec", "tile")
    slots = match_weight.shape[2]
    place = jnp.stack([lax.axis_index("sec"), lax.axis_index("tile"), jnp.int32(n_sec), jnp.int32(n_tile)])

    def flat(s, t):
        return s * n_tile + t

    tile_even = [[flat(s, t), flat(s, t + 1)] for s in range(n_sec) for t in range(0, n_tile, 2)]
    tile_odd = [[flat(s, t), flat(s, t + 1)] for s in range(n_sec) for t in range(1, n_tile - 1, 2)]
    sec_even = [[flat(s, t), flat(s + 1, t)] for s in range(0, n_sec, 2) for t in range(n_tile)]
    sec_odd = [[flat(s, t), flat(s + 1, t)] for s in range(1, n_sec - 1, 2) for t in range(n_tile)]

    def trade(even, odd, even_pairs, odd_pairs):
        swapped = lax.ppermute(odd, axes, [q for a, b in odd_pairs for q in ((a, b), (b, a))])
        gathered = lax.all_gather(even, axes, axis_index_groups=even_pairs)
        return gathered, swapped

    def trade_tiles(even, odd):
        return trade(even, odd, tile_even, tile_odd)

    def trade_secs(even, odd):
        return trade(even, odd, sec_even, sec_odd)

    u = displacement[0].reshape(2, 2, 32, LANES).transpose(0, 2, 1, 3).reshape(2, 64, LANES)
    c = stiffness[0].reshape(2, 32, LANES).transpose(1, 0, 2).reshape(64, LANES)
    off = match_offset[0]
    even, odd, own, ids, u, c = call(
        first_kernel,
        [((32, slots), F32), ((32, slots), F32), ((8, slots), F32), ((16, slots), jnp.int32), ((2, 64, LANES), F32), ((64, LANES), F32)],
        place, match_count, u, c, match_weight[0], off, source_row[0], source_col[0], target_row[0], target_col[0],
        scalars=2,
    )
    even_in, odd_in = trade_tiles(even, odd)
    even, odd = call(lambda *r: pack_kernel(True, *r), [((16, slots), F32)] * 2, place, even_in, odd_in, own)
    near, total = call(
        lambda *r: spring_kernel(True, *r), [((2, 64, LANES), F32), ((64, LANES), F32)], place, even_in, odd_in, u, c
    )
    sec_even_in, sec_odd_in = trade_secs(even, odd)
    u, share, even, odd, own_next = call(
        middle_kernel,
        [((2, 64, LANES), F32), ((64, LANES), F32), ((24, slots), F32), ((24, slots), F32), ((8, slots), F32)],
        place, sec_even_in, sec_odd_in, own, ids, off, u, c, near, total,
    )
    even_in, odd_in = trade_tiles(even, odd)
    even, odd = call(lambda *r: pack_kernel(False, *r), [((8, slots), F32)] * 2, place, even_in, odd_in, own_next)
    (near,) = call(lambda *r: spring_kernel(False, *r), [((2, 64, LANES), F32)], place, even_in, odd_in, u, c)
    sec_even_in, sec_odd_in = trade_secs(even, odd)
    (out,) = call(last_kernel, [((2, 64, LANES), F32)], place, sec_even_in, sec_odd_in, own, ids, off, u, near, share)
    return out.reshape(2, 32, 2, LANES).transpose(0, 2, 1, 3).reshape(1, 2, 2, 32 * LANES)


def solution(mesh):
    placed = (
        P("sec", None, "tile", None),
        P("sec", "tile", None),
        P("sec", "tile", None),
        P("sec", None, "tile", None),
        P("sec", "tile", None),
        P("sec", "tile", None),
        P("sec", "tile", None),
        P("sec", "tile", None),
        P("sec", "tile"),
    )

    def run(*args):
        return body(mesh.shape["sec"], mesh.shape["tile"], *args)

    return jax.shard_map(run, mesh=mesh, in_specs=placed, out_specs=P("sec", None, "tile", None), check_vma=False)
```

time: 167 us -> 53.6 us (0.32)
  the two profiles are of different devices: /device:TPU:415 before, /device:TPU:33 now
where the time goes in v1:
time: 53.6 us; the launch traced here: 53.2 us
  starting transfers between devices  32 us (60%)
  blocking collectives  11.7 us (22%)
  Pallas kernels  7.22 us (13%)
  local copies, waits for them, and re-layouts  2.09 us (4%)
    ppermute x4, starting transfers between devices, trade(): lax.ppermute(odd, axes, [q for a, b in odd_pairs for q in ((a, b), (b, a))])  32 us
    all_gather x4, blocking collectives, trade(): gathered = lax.all_gather(even, axes, axis_index_groups=even_pairs)  11.7 us
    pallas_call x7, Pallas kernels, call(): pl.pallas_call(kernel, out_shape=[jax.ShapeDtypeStruct(s, d) for s, d in...  7.22 us
    unnamed x18, local copies, waits for them, and re-layouts  2.09 us
  transfers between devices with their start and end apart: 4, of which 0 were waited for; matrix products, arithmetic and copies ran while one was open for 0% of the time, Pallas kernels for 3%

profile of v1, /device:TPU:33, one launch (start us, length us, event | category | flops | bytes accessed | tf_op | source)
XLA Modules:
  0.0 53.2 jit_solution(18232985534327969567)
XLA Ops:
  0.0 0.0 copy-start.4
  0.0 0.0 copy-start.3
  0.0 0.0 copy-start.5
  0.0 0.0 copy-start.6
  0.0 0.0 copy-start
  0.0 0.7 %copy-done.4 = f32[1,3,512]{2,0,1:T(1,128)S(1)} copy-done((f32[1,3,512]{2,0,1:T(1,128)S(1)}, f32[1,3,512]{2,0,1:T(1,128)}, u32[]{:S(2)}) %copy-start.4) | copy-done | bytes 6168
  0.7 0.0 copy-done.3
  0.7 0.0 copy-done.5
  0.7 0.0 copy-done.6
  0.7 0.0 copy-start.1
  0.8 0.7 %copy_bitcast_fusion.1 = (s32[3,512]{1,0:T(4,128)S(1)}, s32[3,512]{1,0:T(4,128)S(1)}) fusion(s32[1,3,512]{2,0,1:T(1,128)} %param.16, s32[1,3,512]{2,0,1:T(1,128)} %param.15), kind=kLoop, calls=%fused_computation.1 | loop fusion | bytes 24576
  1.5 0.1 pad_add_fusion.place.r_0_
  1.6 0.0 copy-start.2
  1.6 0.0 copy-done
  1.6 0.0 copy-done.1
  1.6 0.6 %copy-done.2 = s32[1,3]{1,0:T(1,128)S(1)} copy-done((s32[1,3]{1,0:T(1,128)S(1)}, s32[1,3]{1,0:T(1,128)}, u32[]{:S(2)}) %copy-start.2) | copy-done | bytes 36
  2.2 1.2 %shard_map.91 = (f32[32,512]{1,0:T(8,128)S(1)}, f32[32,512]{1,0:T(8,128)S(1)}, f32[8,512]{1,0:T(8,128)S(1)}, s32[16,512]{1,0:T(8,128)S(1)}, f32[2,64,128]{2,1,0:T(8,128)S(1)}, /*index=5*/f32[64,128]{1,0:T(8,128)S(1)}) custom-call(s32[4]{0:T(128)S(1)} %pad_add_fusion.place.r_0_, s32[1,3]{1,0:T(1,128)S(1)} %copy-done.2, f32[2,64,128]{2,1,0:T(8,128)S(1)} %bitcast.44, ...), custom_call_target="tpu_custom_call" | custom-call | tf_op jit(solution)/shard_map/pallas_call | solution.py:243
  3.4 6.4 %collective-permute-start = (f32[32,512]{1,0:T(8,128)S(1)}, f32[32,512]{1,0:T(8,128)S(1)}, u32[]{:S(2)}, u32[]{:S(2)}) collective-permute-start(f32[32,512]{1,0:T(8,128)S(1)} %get-tuple-element.23), channel_id=1, source_target_pairs={{1,2},{2,1},{3,4},{4,3},{5,6},{6,5},{7,8},{8,7},{9,10},{10,9},{11,... | collective-permute-start | bytes 196616 | tf_op jit(solution)/shard_map/ppermute | solution.py:266
  9.8 4.1 %all-gather = f32[64,512]{1,0:T(8,128)S(1)} all-gather(f32[32,512]{1,0:T(8,128)S(1)} %get-tuple-element.22), channel_id=2, replica_groups={{0,1},{2,3},{4,5},{6,7},{8,9},{10,11},{12,13},{14,15},{16,17},{18,19},{..., dimensions={0}, use_global_device_ids=true | all-gather | bytes 196608 | tf_op jit(solution)/shard_map/all_gather | solution.py:267
  13.8 0.0 collective-permute-done.r_2_
  13.9 0.6 %shard_map.92 = (f32[16,512]{1,0:T(8,128)S(1)}, f32[16,512]{1,0:T(8,128)S(1)}) custom-call(s32[4]{0:T(128)S(1)} %pad_add_fusion.place.r_0_, f32[2,32,512]{2,1,0:T(8,128)S(1)} %bitcast.35, f32[32,512]{1,0:T(8,128)S(1)} %collective-permute-done.r_2_, f32[8,512]{1,0:T(8,128)S(1)} %get-tuple-element.24.r_3_.own), custom_call_target="tpu_custom_call" | custom-call | tf_op jit(solution)/shard_map/pallas_call | solution.py:243
  14.4 10.5 %collective-permute-start.1 = (f32[16,512]{1,0:T(8,128)S(1)}, f32[16,512]{1,0:T(8,128)S(1)}, u32[]{:S(2)}, u32[]{:S(2)}) collective-permute-start(f32[16,512]{1,0:T(8,128)S(1)} %get-tuple-element.26), channel_id=1, source_target_pairs={{64,128},{128,64},{65,129},{129,65},{66,130},{130,66},{67,131},{13... | collective-permute-start | bytes 98312 | tf_op jit(solution)/shard_map/ppermute | solution.py:266
  24.9 0.7 %shard_map.93 = (f32[2,64,128]{2,1,0:T(8,128)S(1)}, f32[64,128]{1,0:T(8,128)S(1)}) custom-call(s32[4]{0:T(128)S(1)} %pad_add_fusion.place.r_0_, f32[2,32,512]{2,1,0:T(8,128)S(1)} %bitcast.36, f32[32,512]{1,0:T(8,128)S(1)} %collective-permute-done.r_2_, f32[2,64,128]{2,1,0:T(8,128)S(1)} %get-tuple-element.28.r_3_.u, f32[64,128]{1,0:T(8,128)S(1)} %get-tuple-element.29.r_4_.c), custom_call_target="tpu_custom_call" | custom-call | tf_op jit(solution)/shard_map/pallas_call | solution.py:243
  25.7 1.9 %all-gather.1 = f32[32,512]{1,0:T(8,128)S(1)} all-gather(f32[16,512]{1,0:T(8,128)S(1)} %get-tuple-element.25), channel_id=3, replica_groups={{0,64},{1,65},{2,66},{3,67},{4,68},{5,69},{6,70},{7,71},{8,72},{9,73},{..., dimensions={0}, use_global_device_ids=true | all-gather | bytes 98304 | tf_op jit(solution)/shard_map/all_gather | solution.py:267
  27.5 0.0 collective-permute-done.1.odd_in
  27.5 1.8 %shard_map.94 = (f32[2,64,128]{2,1,0:T(8,128)S(1)}, f32[64,128]{1,0:T(8,128)S(1)}, f32[24,512]{1,0:T(8,128)S(1)}, f32[24,512]{1,0:T(8,128)S(1)}, f32[8,512]{1,0:T(8,128)S(1)}) custom-call(s32[4]{0:T(128)S(1)} %pad_add_fusion.place.r_0_, f32[2,16,512]{2,1,0:T(8,128)S(1)} %bitcast.39, f32[16,512]{1,0:T(8,128)S(1)} %collective-permute-done.1.odd_in, ...), custom_call_target="tpu_custom_call" | custom-call | tf_op jit(solution)/shard_map/pallas_call | solution.py:243
  29.3 5.1 %collective-permute-start.2 = (f32[24,512]{1,0:T(8,128)S(1)}, f32[24,512]{1,0:T(8,128)S(1)}, u32[]{:S(2)}, u32[]{:S(2)}) collective-permute-start(f32[24,512]{1,0:T(8,128)S(1)} %get-tuple-element.33), channel_id=1, source_target_pairs={{1,2},{2,1},{3,4},{4,3},{5,6},{6,5},{7,8},{8,7},{9,10},{10,9},{11,... | collective-permute-start | bytes 147464 | tf_op jit(solution)/shard_map/ppermute | solution.py:266
  34.4 3.9 %all-gather.2 = f32[48,512]{1,0:T(8,128)S(1)} all-gather(f32[24,512]{1,0:T(8,128)S(1)} %get-tuple-element.32), channel_id=4, replica_groups={{0,1},{2,3},{4,5},{6,7},{8,9},{10,11},{12,13},{14,15},{16,17},{18,19},{..., dimensions={0}, use_global_device_ids=true | all-gather | bytes 147456 | tf_op jit(solution)/shard_map/all_gather | solution.py:267
  38.4 0.0 collective-permute-done.2.r_2_
  38.4 0.6 %shard_map.95 = (f32[8,512]{1,0:T(8,128)S(1)}, f32[8,512]{1,0:T(8,128)S(1)}) custom-call(s32[4]{0:T(128)S(1)} %pad_add_fusion.place.r_0_, f32[2,24,512]{2,1,0:T(8,128)S(1)} %bitcast.37, f32[24,512]{1,0:T(8,128)S(1)} %collective-permute-done.2.r_2_, f32[8,512]{1,0:T(8,128)S(1)} %get-tuple-element.34.r_3_), custom_call_target="tpu_custom_call" | custom-call | tf_op jit(solution)/shard_map/pallas_call | solution.py:243
  38.9 10.0 %collective-permute-start.3 = (f32[8,512]{1,0:T(8,128)S(1)}, f32[8,512]{1,0:T(8,128)S(1)}, u32[]{:S(2)}, u32[]{:S(2)}) collective-permute-start(f32[8,512]{1,0:T(8,128)S(1)} %get-tuple-element.36), channel_id=1, source_target_pairs={{64,128},{128,64},{65,129},{129,65},{66,130},{130,66},{67,131},{13... | collective-permute-start | bytes 49160 | tf_op jit(solution)/shard_map/ppermute | solution.py:266
  48.9 0.7 %shard_map.96.near = f32[2,64,128]{2,1,0:T(8,128)S(1)} custom-call(s32[4]{0:T(128)S(1)} %pad_add_fusion.place.r_0_, f32[2,24,512]{2,1,0:T(8,128)S(1)} %bitcast.38, f32[24,512]{1,0:T(8,128)S(1)} %collective-permute-done.2.r_2_, f32[2,64,128]{2,1,0:T(8,128)S(1)} %get-tuple-element.37.r_3_.u, f32[64,128]{1,0:T(8,128)S(1)} %get-tuple-element.29.r_4_.c), custom_call_target="tpu_custom_call" | custom-call | tf_op jit(solution)/shard_map/pallas_call | solution.py:243
  49.6 1.8 %all-gather.3 = f32[16,512]{1,0:T(8,128)S(1)} all-gather(f32[8,512]{1,0:T(8,128)S(1)} %get-tuple-element.35), channel_id=5, replica_groups={{0,64},{1,65},{2,66},{3,67},{4,68},{5,69},{6,70},{7,71},{8,72},{9,73},{..., dimensions={0}, use_global_device_ids=true | all-gather | bytes 49152 | tf_op jit(solution)/shard_map/all_gather | solution.py:267
  51.5 0.0 collective-permute-done.3.odd_in
  51.5 1.8 %shard_map.97 = f32[2,64,128]{2,1,0:T(8,128)} custom-call(s32[4]{0:T(128)S(1)} %pad_add_fusion.place.r_0_, f32[2,8,512]{2,1,0:T(8,128)S(1)} %bitcast.43, f32[8,512]{1,0:T(8,128)S(1)} %collective-permute-done.3.odd_in, f32[8,512]{1,0:T(8,128)S(1)} %get-tuple-element.24.r_3_.own, s32[16,512]{1,0:T(8,128)S(1)} %get-tuple-element.27.ids, ...), custom_call_target="tpu_custom_call" | custom-call | tf_op jit(solution)/shard_map/pallas_call | solution.py:243
  (3 shorter events, 0.0 us)
Async XLA Ops:
  0.0 0.7 %copy-start.4 = (f32[1,3,512]{2,0,1:T(1,128)S(1)}, f32[1,3,512]{2,0,1:T(1,128)}, u32[]{:S(2)}) copy-start(f32[1,3,512]{2,0,1:T(1,128)} %param.11) | copy-start | bytes 18436
  0.0 0.7 %copy-start.3 = (f32[1,2,3,512]{3,1,2,0:T(2,128)S(1)}, f32[1,2,3,512]{3,1,2,0:T(2,128)}, u32[]{:S(2)}) copy-start(f32[1,2,3,512]{3,1,2,0:T(2,128)} %param.12) | copy-start | bytes 36868
  0.0 0.7 %copy-start.5 = (s32[1,3,512]{2,0,1:T(1,128)S(1)}, s32[1,3,512]{2,0,1:T(1,128)}, u32[]{:S(2)}) copy-start(s32[1,3,512]{2,0,1:T(1,128)} %param.14) | copy-start | bytes 18436
  0.0 0.7 %copy-start.6 = (s32[1,3,512]{2,0,1:T(1,128)S(1)}, s32[1,3,512]{2,0,1:T(1,128)}, u32[]{:S(2)}) copy-start(s32[1,3,512]{2,0,1:T(1,128)} %param.13) | copy-start | bytes 18436
  0.0 1.5 %copy-start = (f32[1,2,2,4096]{3,2,1,0:T(2,128)S(1)}, f32[1,2,2,4096]{3,2,1,0:T(2,128)}, u32[]{:S(2)}) copy-start(f32[1,2,2,4096]{3,2,1,0:T(2,128)} %param.9) | copy-start | bytes 196612
  0.7 0.8 %copy-start.1 = (f32[1,2,4096]{2,1,0:T(2,128)S(1)}, f32[1,2,4096]{2,1,0:T(2,128)}, u32[]{:S(2)}) copy-start(f32[1,2,4096]{2,1,0:T(2,128)} %param.10) | copy-start | bytes 98308
  1.6 0.7 %copy-start.2 = (s32[1,3]{1,0:T(1,128)S(1)}, s32[1,3]{1,0:T(1,128)}, u32[]{:S(2)}) copy-start(s32[1,3]{1,0:T(1,128)} %count.1) | copy-start | bytes 40
  3.4 10.5 %collective-permute-start = (f32[32,512]{1,0:T(8,128)S(1)}, f32[32,512]{1,0:T(8,128)S(1)}, u32[]{:S(2)}, u32[]{:S(2)}) collective-permute-start(f32[32,512]{1,0:T(8,128)S(1)} %get-tuple-element.23), channel_id=1, source_target_pairs={{1,2},{2,1},{3,4},{4,3},{5,6},{6,5},{7,8},{8,7},{9,10},{10,9},{11,... | collective-permute-start | bytes 196616 | tf_op jit(solution)/shard_map/ppermute | solution.py:266
  14.4 13.1 %collective-permute-start.1 = (f32[16,512]{1,0:T(8,128)S(1)}, f32[16,512]{1,0:T(8,128)S(1)}, u32[]{:S(2)}, u32[]{:S(2)}) collective-permute-start(f32[16,512]{1,0:T(8,128)S(1)} %get-tuple-element.26), channel_id=1, source_target_pairs={{64,128},{128,64},{65,129},{129,65},{66,130},{130,66},{67,131},{13... | collective-permute-start | bytes 98312 | tf_op jit(solution)/shard_map/ppermute | solution.py:266
  29.3 9.1 %collective-permute-start.2 = (f32[24,512]{1,0:T(8,128)S(1)}, f32[24,512]{1,0:T(8,128)S(1)}, u32[]{:S(2)}, u32[]{:S(2)}) collective-permute-start(f32[24,512]{1,0:T(8,128)S(1)} %get-tuple-element.33), channel_id=1, source_target_pairs={{1,2},{2,1},{3,4},{4,3},{5,6},{6,5},{7,8},{8,7},{9,10},{10,9},{11,... | collective-permute-start | bytes 147464 | tf_op jit(solution)/shard_map/ppermute | solution.py:266
  38.9 12.5 %collective-permute-start.3 = (f32[8,512]{1,0:T(8,128)S(1)}, f32[8,512]{1,0:T(8,128)S(1)}, u32[]{:S(2)}, u32[]{:S(2)}) collective-permute-start(f32[8,512]{1,0:T(8,128)S(1)} %get-tuple-element.36), channel_id=1, source_target_pairs={{64,128},{128,64},{65,129},{129,65},{66,130},{130,66},{67,131},{13... | collective-permute-start | bytes 49160 | tf_op jit(solution)/shard_map/ppermute | solution.py:266

commit v2 on v1

v2 whole, which is shorter than its diff:
```python
import jax
import jax.numpy as jnp
from jax import lax
from jax.experimental import pallas as pl
from jax.experimental.pallas import tpu as pltpu
from jax.sharding import PartitionSpec as P

damping = 0.7
LANES = 128
F32 = jnp.float32
BF16 = jnp.bfloat16
HBM = pl.BlockSpec(memory_space=pltpu.HBM)
VMEM = pl.BlockSpec(memory_space=pltpu.VMEM)


def halves(value):
    high = value.astype(BF16)
    return high, (value - high.astype(F32)).astype(BF16)


def one_hot(index, depth):
    place = lax.broadcasted_iota(jnp.int32, (depth, index.shape[1]), 0)
    return place == index


def gather(table, lane_hot, block_mask):
    blocks = block_mask.shape[0]
    picked = jnp.dot(table, jnp.concatenate([lane_hot, lane_hot], axis=0), preferred_element_type=F32)
    return [
        jnp.sum(jnp.where(block_mask, picked[i * blocks : (i + 1) * blocks], 0.0), axis=0, keepdims=True)
        for i in range(picked.shape[0] // blocks)
    ]


def table_of(fields):
    high, low = halves(jnp.concatenate(fields, axis=0))
    return jnp.concatenate([high, low], axis=1)


def scatter(values, lane_hot, block_hot):
    parts = [halves(v) for v in values]
    left = jnp.concatenate([block_hot * p[k] for k in range(2) for p in parts], axis=0)
    return lax.dot_general(left, lane_hot, (((1,), (1,)), ((), ())), preferred_element_type=F32)


def wide(block):
    return jnp.concatenate([block[8 * i : 8 * i + 8] for i in range(4)], axis=1)


def narrow(rows):
    return jnp.concatenate([rows[:, LANES * i : LANES * (i + 1)] for i in range(4)], axis=0)


def side_sum(block):
    count = block.shape[0]
    lane = lax.broadcasted_iota(jnp.int32, block.shape, 1)
    row = lax.broadcasted_iota(jnp.int32, block.shape, 0)
    before = pltpu.roll(block, 1, 1)
    carried = jnp.where(row == 0, 0.0, pltpu.roll(before, 1, 0))
    before = jnp.where(lane == 0, carried, before)
    after = pltpu.roll(block, LANES - 1, 1)
    carried = jnp.where(row == count - 1, 0.0, pltpu.roll(after, count - 1, 0))
    after = jnp.where(lane == LANES - 1, carried, after)
    return before + after


def stencil(above, first, second, below):
    sides = [side_sum(b) for b in (above, first, second, below)]
    upper = first + 0.5 * sides[1]
    lower = second + 0.5 * sides[2]
    return jnp.concatenate(
        [
            above + 0.5 * sides[0] + lower + sides[1],
            upper + below + 0.5 * sides[3] + sides[2],
        ],
        axis=0,
    )


def rows_of(ref, lead=()):
    return [ref[lead + (pl.ds(r, 32, 2), slice(None))] for r in range(2)]


def fill(ref, rows):
    pad = (-len(rows)) % 8
    ref[...] = jnp.concatenate(rows + [jnp.zeros_like(rows[0])] * pad, axis=0)


def send_tiles(odd_tile, left, right, even_ref, odd_ref):
    even_ref[...] = jnp.where(odd_tile, left, right)
    odd_ref[...] = jnp.where(odd_tile, right, left)


def tile_message(halo, slot_rows):
    pad = (-len(slot_rows)) % 8
    rows = [wide(h) for h in halo] + slot_rows + [jnp.zeros_like(slot_rows[0])] * pad
    return jnp.concatenate(rows, axis=0)


def spot():
    return lax.axis_index("sec"), lax.axis_index("tile")


def first_kernel(n_sec, n_tile, *refs):
    far, (even_msg, odd_msg, own, ids, uo, co), held, sems = refs[:9], refs[9:15], refs[15:24], refs[24]
    copies = [pltpu.make_async_copy(f, h, sems.at[i]) for i, (f, h) in enumerate(zip(far, held))]
    for copy in copies:
        copy.start()
    for copy in copies:
        copy.wait()
    count, u, c, w, off, srow, scol, trow, tcol = held
    sec, tile = spot()
    field = [jnp.concatenate(rows_of(u, (i,)), axis=0) for i in range(2)]
    stiff = jnp.concatenate(rows_of(c), axis=0)
    for i in range(2):
        uo[i] = field[i]
    co[...] = stiff
    table = table_of(field)
    slot = lax.broadcasted_iota(jnp.int32, (1, w.shape[2]), 1)
    sources, targets, blocks, lanes, pulls = [], [], [], [], []
    for g in range(3):
        dest = tile + g - 1
        open_group = (sec < n_sec - 1) & (dest >= 0) & (dest < n_tile)
        limit = jnp.where(open_group, count[0:1, g : g + 1], 0)
        weight = jnp.where(slot < limit, w[g], 0.0)
        col = scol[g]
        block, lane = srow[g] * 32 + (col >> 7), col & 127
        blocks.append(block)
        lanes.append(lane)
        got = gather(table, one_hot(lane, LANES).astype(BF16), one_hot(block, 64))
        sources.append([weight * (got[i] - off[g, i : i + 1]) for i in range(2)] + [weight])
    for k in range(3):
        col = tcol[k]
        block, lane = trow[k] * 32 + (col >> 7), col & 127
        blocks.append(block)
        lanes.append(lane)
        targets.append(gather(table, one_hot(lane, LANES).astype(BF16), one_hot(block, 64)))
    halo = [stiff * field[0], stiff * field[1], stiff]
    left = tile_message([h[:32] for h in halo], sources[0] + targets[0])
    right = tile_message([h[32:] for h in halo], sources[2] + targets[2])
    send_tiles((tile & 1) == 1, left, right, even_msg, odd_msg)
    offsets = [off[g, i : i + 1] for g in range(3) for i in range(2)]
    fill(own, sources[1] + targets[1] + [s[2] for s in sources] + offsets)
    fill(ids, blocks + lanes)


def both_sides(even_in, odd_in, rows):
    parity = spot()[1] & 1
    even = even_in[1 - parity, rows, :]
    odd = odd_in[rows, :]
    return jnp.where(parity == 1, even, odd), jnp.where(parity == 1, odd, even)


def pack_kernel(first, even_in, odd_in, own, even_msg, odd_msg):
    base = 24 if first else 16
    n_src = 3 if first else 2
    left, right = both_sides(even_in, odd_in, slice(base, base + 8))
    own_rows = own[0:8]
    source = [m[i : i + 1] for m in (left, own_rows, right) for i in range(n_src)]
    target = [m[n_src + i : n_src + i + 1] for m in (left, own_rows, right) for i in range(2)]
    size = even_msg.shape[0]
    zero = jnp.zeros_like(source[0])
    source = jnp.concatenate(source + [zero] * (size - len(source)), axis=0)
    target = jnp.concatenate(target + [zero] * (size - len(target)), axis=0)
    send_tiles((spot()[0] & 1) == 1, target, source, even_msg, odd_msg)


def springs(fields, even_in, odd_in):
    up, down = both_sides(even_in, odd_in, slice(0, 8 * len(fields)))
    return [
        stencil(narrow(up[8 * i : 8 * i + 8]), f[:32], f[32:], narrow(down[8 * i : 8 * i + 8]))
        for i, f in enumerate(fields)
    ]


def arrivals(even_in, odd_in):
    parity = spot()[0] & 1
    even, odd = even_in[1 - parity], odd_in[parity]
    return jnp.where(parity == 1, even, odd), jnp.where(parity == 1, odd, even)


def offset_rows(own):
    return lambda g, i: own[8 + 2 * g + i : 9 + 2 * g + i, :]


def hots_of(ids):
    return [(one_hot(ids[6 + g : 7 + g], LANES).astype(BF16), one_hot(ids[g : g + 1], 64)) for g in range(6)]


def middle_kernel(
    even_tile, odd_tile, even_sec, odd_sec, own, ids, u, c, u_out, total_out, even_msg, odd_msg, own_out
):
    source_in, target_in = arrivals(even_sec, odd_sec)
    off = offset_rows(own)
    hots = hots_of(ids[...])
    weights = [own[5 + g : 6 + g, :] for g in range(3)]
    acc = jnp.zeros((384, LANES), F32)
    for g in range(6):
        if g < 3:
            vals = [weights[g] * (target_in[2 * g + i : 2 * g + i + 1] + off(g, i)) for i in range(2)] + [weights[g]]
        else:
            vals = [source_in[3 * (g - 3) + i : 3 * (g - 3) + i + 1] for i in range(3)]
        acc = acc + scatter(vals, hots[g][0], hots[g][1].astype(BF16))
    acc = acc[:192] + acc[192:]
    stiff = c[...]
    near = springs([stiff * u[0], stiff * u[1], stiff], even_tile, odd_tile)
    share = damping / (stiff * near[2] + acc[128:192])
    total_out[...] = share
    field = [(1.0 - damping) * u[i] + (stiff * near[i] + acc[64 * i : 64 * i + 64]) * share for i in range(2)]
    for i in range(2):
        u_out[i] = field[i]
    table = table_of(field)
    got = [gather(table, *h) for h in hots]
    sources = [[weights[g] * (got[g][i] - off(g, i)) for i in range(2)] for g in range(3)]
    targets = got[3:]
    halo = [stiff * field[0], stiff * field[1]]
    left = tile_message([h[:32] for h in halo], sources[0] + targets[0])
    right = tile_message([h[32:] for h in halo], sources[2] + targets[2])
    send_tiles((spot()[1] & 1) == 1, left, right, even_msg, odd_msg)
    fill(own_out, sources[1] + targets[1])


def last_kernel(even_tile, odd_tile, even_sec, odd_sec, own, ids, u, c, share, out):
    source_in, target_in = arrivals(even_sec, odd_sec)
    off = offset_rows(own)
    hots = hots_of(ids[...])
    acc = jnp.zeros((256, LANES), F32)
    for g in range(6):
        if g < 3:
            weight = own[5 + g : 6 + g, :]
            vals = [weight * (target_in[2 * g + i : 2 * g + i + 1] + off(g, i)) for i in range(2)]
        else:
            vals = [source_in[2 * (g - 3) + i : 2 * (g - 3) + i + 1] for i in range(2)]
        acc = acc + scatter(vals, hots[g][0], hots[g][1].astype(BF16))
    acc = acc[:128] + acc[128:]
    stiff = c[...]
    near = springs([stiff * u[0], stiff * u[1]], even_tile, odd_tile)
    for i in range(2):
        new = (1.0 - damping) * u[i] + (stiff * near[i] + acc[64 * i : 64 * i + 64]) * share[...]
        for r in range(2):
            out[i, pl.ds(r, 32, 2), :] = new[32 * r : 32 * r + 32]


def call(kernel, shapes, *args, held=False):
    scratch = [pltpu.VMEM(a.shape, a.dtype) for a in args] + [pltpu.SemaphoreType.DMA((len(args),))]
    return pl.pallas_call(
        kernel,
        out_shape=[jax.ShapeDtypeStruct(s, d) for s, d in shapes],
        in_specs=[HBM if held else VMEM] * len(args),
        out_specs=[VMEM] * len(shapes),
        scratch_shapes=scratch if held else [],
        compiler_params=pltpu.CompilerParams(vmem_limit_bytes=32 * 1024 * 1024),
    )(*([pltpu.with_memory_space_constraint(a, pltpu.HBM) for a in args] if held else args))


def body(n_sec, n_tile, displacement, stiffness, match_weight, match_offset, source_row, source_col, target_row, target_col, match_count):
    axes = ("sec", "tile")
    slots = match_weight.shape[2]

    def flat(s, t):
        return s % n_sec * n_tile + t

    tile_even = [[flat(s, t), flat(s, t + 1)] for s in range(n_sec) for t in range(0, n_tile, 2)]
    tile_odd = [[flat(s, t), flat(s, t + 1)] for s in range(n_sec) for t in range(1, n_tile - 1, 2)]
    sec_even = [[flat(s, t), flat(s + 1, t)] for s in range(0, n_sec, 2) for t in range(n_tile)]
    sec_odd = [[flat(s, t), flat(s + 1, t)] for s in range(1, n_sec, 2) for t in range(n_tile)]

    def trade_tiles(even, odd):
        swapped = lax.ppermute(odd, axes, [q for a, b in tile_odd for q in ((a, b), (b, a))])
        return lax.all_gather(even, axes, axis_index_groups=tile_even), swapped

    def trade_secs(even, odd):
        even_in = lax.all_gather(even, axes, axis_index_groups=sec_even)
        odd, even_in = lax.optimization_barrier((odd, even_in))
        return even_in, lax.all_gather(odd, axes, axis_index_groups=sec_odd)

    u = displacement[0].reshape(2, 2, 32, LANES).transpose(0, 2, 1, 3).reshape(2, 64, LANES)
    c = stiffness[0].reshape(2, 32, LANES).transpose(1, 0, 2).reshape(64, LANES)
    w, srow, scol, trow, tcol = [a.transpose(1, 0, 2) for a in (match_weight, source_row, source_col, target_row, target_col)]
    off = match_offset[0].transpose(1, 0, 2)
    even, odd, own, ids, u, c = call(
        lambda *r: first_kernel(n_sec, n_tile, *r),
        [((32, slots), F32), ((32, slots), F32), ((16, slots), F32), ((16, slots), jnp.int32), ((2, 64, LANES), F32), ((64, LANES), F32)],
        match_count, u, c, w, off, srow, scol, trow, tcol,
        held=True,
    )
    tiles_in = trade_tiles(even, odd)
    even, odd = call(lambda *r: pack_kernel(True, *r), [((16, slots), F32)] * 2, *tiles_in, own)
    u, share, even, odd, own_next = call(
        middle_kernel,
        [((2, 64, LANES), F32), ((64, LANES), F32), ((24, slots), F32), ((24, slots), F32), ((8, slots), F32)],
        *tiles_in, *trade_secs(even, odd), own, ids, u, c,
    )
    tiles_in = trade_tiles(even, odd)
    even, odd = call(lambda *r: pack_kernel(False, *r), [((8, slots), F32)] * 2, *tiles_in, own_next)
    (out,) = call(last_kernel, [((2, 64, LANES), F32)], *tiles_in, *trade_secs(even, odd), own, ids, u, c, share)
    return out.reshape(2, 32, 2, LANES).transpose(0, 2, 1, 3).reshape(1, 2, 2, 32 * LANES)


def solution(mesh):
    placed = (
        P("sec", None, "tile", None),
        P("sec", "tile", None),
        P("sec", "tile", None),
        P("sec", None, "tile", None),
        P("sec", "tile", None),
        P("sec", "tile", None),
        P("sec", "tile", None),
        P("sec", "tile", None),
        P("sec", "tile"),
    )

    def run(*args):
        return body(mesh.shape["sec"], mesh.shape["tile"], *args)

    return jax.shard_map(run, mesh=mesh, in_specs=placed, out_specs=P("sec", None, "tile", None), check_vma=False)
```

time: 53.6 us -> 50.9 us (0.950)
  blocking collectives: 11.7 us -> 34.7 us
  starting transfers between devices: 32 us -> 11.6 us
  Pallas kernels: 7.22 us -> 4.08 us
  local copies, waits for them, and re-layouts: 2.09 us -> 0 us
    all_gather x4 -> x6, blocking collectives: 11.7 us -> 34.7 us  [the longest x2 17.1 us: trade_secs(): return (even_in, lax.all_gather(odd, axes, axis_index_groups=sec_odd))]
    ppermute x4 -> x2, starting transfers between devices: 32 us -> 11.6 us  [trade_tiles(): lax.ppermute(odd, axes, [q for a, b in tile_odd for q in ((a, b), (b, a))])]
    pallas_call x7 -> x5, Pallas kernels: 7.22 us -> 4.08 us  [call(): pl.pallas_call(kernel, out_shape=[jax.ShapeDtypeStruct(s, d) for s, d in...]
    unnamed x18 -> x0, local copies, waits for them, and re-layouts: 2.09 us -> none
  transfers between devices with their start and end apart: 4 -> 2, of which waited for: 0 -> 1; matrix products, arithmetic and copies ran while one was open for 0% -> 0% of each run, Pallas kernels for 3% -> 0%
where the time goes in v2:
time: 50.9 us; the launch traced here: 50.6 us
  blocking collectives  34.7 us (68%)
  starting transfers between devices  11.6 us (23%)
  Pallas kernels  4.08 us (8%)
    all_gather x2, blocking collectives, trade_secs(): return (even_in, lax.all_gather(odd, axes, axis_index_groups=sec_odd))  17.1 us
    ppermute x2, starting transfers between devices, trade_tiles(): lax.ppermute(odd, axes, [q for a, b in tile_odd for q in ((a, b), (b, a))])  11.6 us
    all_gather x2, blocking collectives, trade_secs(): even_in = lax.all_gather(even, axes, axis_index_groups=sec_even)  9.85 us
    all_gather x2, blocking collectives, trade_tiles(): return (lax.all_gather(even, axes, axis_index_groups=tile_even), swapped)  7.71 us
    pallas_call x5, Pallas kernels, call(): pl.pallas_call(kernel, out_shape=[jax.ShapeDtypeStruct(s, d) for s, d in...  4.08 us
  transfers between devices with their start and end apart: 2, of which 1 were waited for; matrix products, arithmetic and copies ran while one was open for 0% of the time, Pallas kernels for 0%

profile of v2, /device:TPU:33, one launch (start us, length us, event | category | flops | bytes accessed | tf_op | source)
XLA Modules:
  0.0 50.6 jit_solution(5289199418426541676)
XLA Ops:
  0.0 1.6 %shard_map.91 = (f32[32,512]{1,0:T(8,128)S(1)}, f32[32,512]{1,0:T(8,128)S(1)}, f32[16,512]{1,0:T(8,128)S(1)}, s32[16,512]{1,0:T(8,128)S(1)}, f32[2,64,128]{2,1,0:T(8,128)S(1)}, /*index=5*/f32[64,128]{1,0:T(8,128)S(1)}) custom-call(s32[1,3]{1,0:T(1,128)} %r_0_.1, f32[2,64,128]{2,1,0:T(8,128)} %bitcast.37, f32[64,128]{1,0:T(8,128)} %bitcast.38, ...), custom_call_target="tpu_custom_call" | custom-call | tf_op jit(solution)/shard_map/pallas_call | solution.py:246
  1.6 6.4 %collective-permute-start = (f32[32,512]{1,0:T(8,128)S(1)}, f32[32,512]{1,0:T(8,128)S(1)}, u32[]{:S(2)}, u32[]{:S(2)}) collective-permute-start(f32[32,512]{1,0:T(8,128)S(1)} %get-tuple-element.25), channel_id=1, source_target_pairs={{1,2},{2,1},{3,4},{4,3},{5,6},{6,5},{7,8},{8,7},{9,10},{10,9},{11,... | collective-permute-start | bytes 196616 | tf_op jit(solution)/shard_map/ppermute | solution.py:269
  8.0 4.1 %all-gather = f32[64,512]{1,0:T(8,128)S(1)} all-gather(f32[32,512]{1,0:T(8,128)S(1)} %get-tuple-element.24), channel_id=2, replica_groups={{0,1},{2,3},{4,5},{6,7},{8,9},{10,11},{12,13},{14,15},{16,17},{18,19},{..., dimensions={0}, use_global_device_ids=true | all-gather | bytes 196608 | tf_op jit(solution)/shard_map/all_gather | solution.py:270
  12.0 0.0 collective-permute-done.r_1_.odd_tile
  12.1 3.3 %all-gather.1 = f32[32,512]{1,0:T(8,128)S(1)} all-gather(f32[16,512]{1,0:T(8,128)S(1)} %get-tuple-element.28), channel_id=3, replica_groups={{0,64},{1,65},{2,66},{3,67},{4,68},{5,69},{6,70},{7,71},{8,72},{9,73},{..., dimensions={0}, use_global_device_ids=true | all-gather | bytes 98304 | tf_op jit(solution)/shard_map/all_gather | solution.py:273
  15.4 9.4 %all-gather.2 = f32[32,512]{1,0:T(8,128)S(1)} all-gather(f32[16,512]{1,0:T(8,128)S(1)} %get-tuple-element.30), channel_id=4, replica_groups={{64,128},{65,129},{66,130},{67,131},{68,132},{69,133},{70,134},{71,135}..., dimensions={0}, use_global_device_ids=true | all-gather | bytes 98304 | tf_op jit(solution)/shard_map/all_gather | solution.py:275
  24.8 1.2 %shard_map.93 = (f32[2,64,128]{2,1,0:T(8,128)S(1)}, f32[64,128]{1,0:T(8,128)S(1)}, f32[24,512]{1,0:T(8,128)S(1)}, f32[24,512]{1,0:T(8,128)S(1)}, f32[8,512]{1,0:T(8,128)S(1)}) custom-call(f32[2,32,512]{2,1,0:T(8,128)S(1)} %bitcast.30, f32[32,512]{1,0:T(8,128)S(1)} %collective-permute-done.r_1_.odd_tile, f32[2,16,512]{2,1,0:T(8,128)S(1)} %bitcast.33, ...), custom_call_target="tpu_custom_call" | custom-call | tf_op jit(solution)/shard_map/pallas_call | solution.py:246
  26.0 5.2 %collective-permute-start.1 = (f32[24,512]{1,0:T(8,128)S(1)}, f32[24,512]{1,0:T(8,128)S(1)}, u32[]{:S(2)}, u32[]{:S(2)}) collective-permute-start(f32[24,512]{1,0:T(8,128)S(1)} %get-tuple-element.35), channel_id=1, source_target_pairs={{1,2},{2,1},{3,4},{4,3},{5,6},{6,5},{7,8},{8,7},{9,10},{10,9},{11,... | collective-permute-start | bytes 147464 | tf_op jit(solution)/shard_map/ppermute | solution.py:269
  31.2 3.6 %all-gather.3 = f32[48,512]{1,0:T(8,128)S(1)} all-gather(f32[24,512]{1,0:T(8,128)S(1)} %get-tuple-element.34), channel_id=5, replica_groups={{0,1},{2,3},{4,5},{6,7},{8,9},{10,11},{12,13},{14,15},{16,17},{18,19},{..., dimensions={0}, use_global_device_ids=true | all-gather | bytes 147456 | tf_op jit(solution)/shard_map/all_gather | solution.py:270
  34.8 0.2 collective-permute-done.1.r_1_.odd_tile
  35.1 6.5 %all-gather.4 = f32[16,512]{1,0:T(8,128)S(1)} all-gather(f32[8,512]{1,0:T(8,128)S(1)} %get-tuple-element.38), channel_id=6, replica_groups={{0,64},{1,65},{2,66},{3,67},{4,68},{5,69},{6,70},{7,71},{8,72},{9,73},{..., dimensions={0}, use_global_device_ids=true | all-gather | bytes 49152 | tf_op jit(solution)/shard_map/all_gather | solution.py:273
  41.6 7.8 %all-gather.5 = f32[16,512]{1,0:T(8,128)S(1)} all-gather(f32[8,512]{1,0:T(8,128)S(1)} %get-tuple-element.40), channel_id=7, replica_groups={{64,128},{65,129},{66,130},{67,131},{68,132},{69,133},{70,134},{71,135}..., dimensions={0}, use_global_device_ids=true | all-gather | bytes 49152 | tf_op jit(solution)/shard_map/all_gather | solution.py:275
  49.4 1.2 %shard_map.95 = f32[2,64,128]{2,1,0:T(8,128)} custom-call(f32[2,24,512]{2,1,0:T(8,128)S(1)} %bitcast.32, f32[24,512]{1,0:T(8,128)S(1)} %collective-permute-done.1.r_1_.odd_tile, f32[2,8,512]{2,1,0:T(8,128)S(1)} %bitcast.35, f32[2,8,512]{2,1,0:T(8,128)S(1)} %bitcast.36, f32[16,512]{1,0:T(8,128)S(1)} %get-tuple-element.26.r_2_.own, ...), custom_call_target="tpu_custom_call" | custom-call | tf_op jit(solution)/shard_map/pallas_call | solution.py:246
  (2 shorter events, 0.0 us)
Async XLA Ops:
  1.6 10.5 %collective-permute-start = (f32[32,512]{1,0:T(8,128)S(1)}, f32[32,512]{1,0:T(8,128)S(1)}, u32[]{:S(2)}, u32[]{:S(2)}) collective-permute-start(f32[32,512]{1,0:T(8,128)S(1)} %get-tuple-element.25), channel_id=1, source_target_pairs={{1,2},{2,1},{3,4},{4,3},{5,6},{6,5},{7,8},{8,7},{9,10},{10,9},{11,... | collective-permute-start | bytes 196616 | tf_op jit(solution)/shard_map/ppermute | solution.py:269
  26.0 9.1 %collective-permute-start.1 = (f32[24,512]{1,0:T(8,128)S(1)}, f32[24,512]{1,0:T(8,128)S(1)}, u32[]{:S(2)}, u32[]{:S(2)}) collective-permute-start(f32[24,512]{1,0:T(8,128)S(1)} %get-tuple-element.35), channel_id=1, source_target_pairs={{1,2},{2,1},{3,4},{4,3},{5,6},{6,5},{7,8},{8,7},{9,10},{10,9},{11,... | collective-permute-start | bytes 147464 | tf_op jit(solution)/shard_map/ppermute | solution.py:269

commit v3 on v2

--- a/solution.py
+++ b/solution.py
@@ -135,13 +135,21 @@
         blocks.append(block)
         lanes.append(lane)
         targets.append(gather(table, one_hot(lane, LANES).astype(BF16), one_hot(block, 64)))
-    halo = [stiff * field[0], stiff * field[1], stiff]
-    left = tile_message([h[:32] for h in halo], sources[0] + targets[0])
-    right = tile_message([h[32:] for h in halo], sources[2] + targets[2])
-    send_tiles((tile & 1) == 1, left, right, even_msg, odd_msg)
+    send_secs(sources, targets, even_msg, odd_msg)
     offsets = [off[g, i : i + 1] for g in range(3) for i in range(2)]
-    fill(own, sources[1] + targets[1] + [s[2] for s in sources] + offsets)
+    zero = jnp.zeros_like(offsets[0])
+    fill(own, [zero] * 5 + [s[2] for s in sources] + offsets)
     fill(ids, blocks + lanes)
+
+
+def send_secs(sources, targets, even_msg, odd_msg):
+    size = even_msg.shape[0]
+    source = [r for s in sources for r in s]
+    target = [r for s in targets for r in s]
+    zero = jnp.zeros_like(source[0])
+    source = jnp.concatenate(source + [zero] * (size - len(source)), axis=0)
+    target = jnp.concatenate(target + [zero] * (size - len(target)), axis=0)
+    send_tiles((spot()[0] & 1) == 1, target, source, even_msg, odd_msg)
 
 
 def both_sides(even_in, odd_in, rows):
@@ -151,18 +159,30 @@
     return jnp.where(parity == 1, even, odd), jnp.where(parity == 1, odd, even)
 
 
-def pack_kernel(first, even_in, odd_in, own, even_msg, odd_msg):
+def pack_kernel(first, even_in, odd_in, u, c, even_msg, odd_msg, mid):
+    n_src = 3 if first else 2
+    source, target = arrivals(even_in, odd_in)
+    rows = [
+        [source[n_src * g + i : n_src * g + i + 1] for i in range(n_src)]
+        + [target[2 * g + i : 2 * g + i + 1] for i in range(2)]
+        for g in range(3)
+    ]
+    stiff = c[...]
+    halo = [stiff * u[0], stiff * u[1]] + ([stiff] if first else [])
+    left = tile_message([h[:32] for h in halo], rows[0])
+    right = tile_message([h[32:] for h in halo], rows[2])
+    send_tiles((spot()[1] & 1) == 1, left, right, even_msg, odd_msg)
+    fill(mid, rows[1])
+
+
+def slot_arrivals(first, even_in, odd_in, mid):
     base = 24 if first else 16
     n_src = 3 if first else 2
     left, right = both_sides(even_in, odd_in, slice(base, base + 8))
-    own_rows = own[0:8]
-    source = [m[i : i + 1] for m in (left, own_rows, right) for i in range(n_src)]
-    target = [m[n_src + i : n_src + i + 1] for m in (left, own_rows, right) for i in range(2)]
-    size = even_msg.shape[0]
-    zero = jnp.zeros_like(source[0])
-    source = jnp.concatenate(source + [zero] * (size - len(source)), axis=0)
-    target = jnp.concatenate(target + [zero] * (size - len(target)), axis=0)
-    send_tiles((spot()[0] & 1) == 1, target, source, even_msg, odd_msg)
+    sides = (left, mid[...], right)
+    source = [m[i : i + 1] for m in sides for i in range(n_src)]
+    target = [m[n_src + i : n_src + i + 1] for m in sides for i in range(2)]
+    return source, target
 
 
 def springs(fields, even_in, odd_in):
@@ -174,9 +194,11 @@
 
 
 def arrivals(even_in, odd_in):
-    parity = spot()[0] & 1
+    sec = spot()[0]
+    parity = sec & 1
     even, odd = even_in[1 - parity], odd_in[parity]
-    return jnp.where(parity == 1, even, odd), jnp.where(parity == 1, odd, even)
+    source, target = jnp.where(parity == 1, even, odd), jnp.where(parity == 1, odd, even)
+    return jnp.where(sec == 0, 0.0, source), target
 
 
 def offset_rows(own):
@@ -188,18 +210,18 @@
 
 
 def middle_kernel(
-    even_tile, odd_tile, even_sec, odd_sec, own, ids, u, c, u_out, total_out, even_msg, odd_msg, own_out
+    even_tile, odd_tile, mid, own, ids, u, c, u_out, total_out, even_msg, odd_msg
 ):
-    source_in, target_in = arrivals(even_sec, odd_sec)
+    source_in, target_in = slot_arrivals(True, even_tile, odd_tile, mid)
     off = offset_rows(own)
     hots = hots_of(ids[...])
     weights = [own[5 + g : 6 + g, :] for g in range(3)]
     acc = jnp.zeros((384, LANES), F32)
     for g in range(6):
         if g < 3:
-            vals = [weights[g] * (target_in[2 * g + i : 2 * g + i + 1] + off(g, i)) for i in range(2)] + [weights[g]]
+            vals = [weights[g] * (target_in[2 * g + i] + off(g, i)) for i in range(2)] + [weights[g]]
         else:
-            vals = [source_in[3 * (g - 3) + i : 3 * (g - 3) + i + 1] for i in range(3)]
+            vals = [source_in[3 * (g - 3) + i] for i in range(3)]
         acc = acc + scatter(vals, hots[g][0], hots[g][1].astype(BF16))
     acc = acc[:192] + acc[192:]
     stiff = c[...]
@@ -212,25 +234,20 @@
     table = table_of(field)
     got = [gather(table, *h) for h in hots]
     sources = [[weights[g] * (got[g][i] - off(g, i)) for i in range(2)] for g in range(3)]
-    targets = got[3:]
-    halo = [stiff * field[0], stiff * field[1]]
-    left = tile_message([h[:32] for h in halo], sources[0] + targets[0])
-    right = tile_message([h[32:] for h in halo], sources[2] + targets[2])
-    send_tiles((spot()[1] & 1) == 1, left, right, even_msg, odd_msg)
-    fill(own_out, sources[1] + targets[1])
-
-
-def last_kernel(even_tile, odd_tile, even_sec, odd_sec, own, ids, u, c, share, out):
-    source_in, target_in = arrivals(even_sec, odd_sec)
+    send_secs(sources, got[3:], even_msg, odd_msg)
+
+
+def last_kernel(even_tile, odd_tile, mid, own, ids, u, c, share, out):
+    source_in, target_in = slot_arrivals(False, even_tile, odd_tile, mid)
     off = offset_rows(own)
     hots = hots_of(ids[...])
     acc = jnp.zeros((256, LANES), F32)
     for g in range(6):
         if g < 3:
             weight = own[5 + g : 6 + g, :]
-            vals = [weight * (target_in[2 * g + i : 2 * g + i + 1] + off(g, i)) for i in range(2)]
+            vals = [weight * (target_in[2 * g + i] + off(g, i)) for i in range(2)]
         else:
-            vals = [source_in[2 * (g - 3) + i : 2 * (g - 3) + i + 1] for i in range(2)]
+            vals = [source_in[2 * (g - 3) + i] for i in range(2)]
         acc = acc + scatter(vals, hots[g][0], hots[g][1].astype(BF16))
     acc = acc[:128] + acc[128:]
     stiff = c[...]
@@ -263,7 +280,8 @@
     tile_even = [[flat(s, t), flat(s, t + 1)] for s in range(n_sec) for t in range(0, n_tile, 2)]
     tile_odd = [[flat(s, t), flat(s, t + 1)] for s in range(n_sec) for t in range(1, n_tile - 1, 2)]
     sec_even = [[flat(s, t), flat(s + 1, t)] for s in range(0, n_sec, 2) for t in range(n_tile)]
-    sec_odd = [[flat(s, t), flat(s + 1, t)] for s in range(1, n_sec, 2) for t in range(n_tile)]
+    sec_odd = [[flat(s, t), flat(s + 1, t)] for s in range(1, n_sec - 1, 2) for t in range(n_tile)]
+    sec_odd += [[flat(s, t), flat(s, t + 1)] for s in (0, n_sec - 1) for t in range(0, n_tile, 2)]
 
     def trade_tiles(even, odd):
         swapped = lax.ppermute(odd, axes, [q for a, b in tile_odd for q in ((a, b), (b, a))])
@@ -280,20 +298,22 @@
     off = match_offset[0].transpose(1, 0, 2)
     even, odd, own, ids, u, c = call(
         lambda *r: first_kernel(n_sec, n_tile, *r),
-        [((32, slots), F32), ((32, slots), F32), ((16, slots), F32), ((16, slots), jnp.int32), ((2, 64, LANES), F32), ((64, LANES), F32)],
+        [((16, slots), F32), ((16, slots), F32), ((16, slots), F32), ((16, slots), jnp.int32), ((2, 64, LANES), F32), ((64, LANES), F32)],
         match_count, u, c, w, off, srow, scol, trow, tcol,
         held=True,
     )
-    tiles_in = trade_tiles(even, odd)
-    even, odd = call(lambda *r: pack_kernel(True, *r), [((16, slots), F32)] * 2, *tiles_in, own)
-    u, share, even, odd, own_next = call(
+    even, odd, mid = call(
+        lambda *r: pack_kernel(True, *r), [((32, slots), F32)] * 2 + [((8, slots), F32)], *trade_secs(even, odd), u, c
+    )
+    u, share, even, odd = call(
         middle_kernel,
-        [((2, 64, LANES), F32), ((64, LANES), F32), ((24, slots), F32), ((24, slots), F32), ((8, slots), F32)],
-        *tiles_in, *trade_secs(even, odd), own, ids, u, c,
-    )
-    tiles_in = trade_tiles(even, odd)
-    even, odd = call(lambda *r: pack_kernel(False, *r), [((8, slots), F32)] * 2, *tiles_in, own_next)
-    (out,) = call(last_kernel, [((2, 64, LANES), F32)], *tiles_in, *trade_secs(even, odd), own, ids, u, c, share)
+        [((2, 64, LANES), F32), ((64, LANES), F32), ((8, slots), F32), ((8, slots), F32)],
+        *trade_tiles(even, odd), mid, own, ids, u, c,
+    )
+    even, odd, mid = call(
+        lambda *r: pack_kernel(False, *r), [((24, slots), F32)] * 2 + [((8, slots), F32)], *trade_secs(even, odd), u, c
+    )
+    (out,) = call(last_kernel, [((2, 64, LANES), F32)], *trade_tiles(even, odd), mid, own, ids, u, c, share)
     return out.reshape(2, 32, 2, LANES).transpose(0, 2, 1, 3).reshape(1, 2, 2, 32 * LANES)
 
 

time: 50.9 us -> 47.1 us (0.925)
  the two profiles are of different devices: /device:TPU:33 before, /device:TPU:320 now
where the time goes in v3:
time: 47.1 us; the launch traced here: 46.8 us
  blocking collectives  29 us (62%)
  starting transfers between devices  13.7 us (29%)
  Pallas kernels  4.08 us (9%)
    all_gather x2, blocking collectives, trade_secs(): return (even_in, lax.all_gather(odd, axes, axis_index_groups=sec_odd))  15.6 us
    ppermute x2, starting transfers between devices, trade_tiles(): lax.ppermute(odd, axes, [q for a, b in tile_odd for q in ((a, b), (b, a))])  13.7 us
    all_gather x2, blocking collectives, trade_tiles(): return (lax.all_gather(even, axes, axis_index_groups=tile_even), swapped)  9.71 us
    pallas_call x5, Pallas kernels, call(): pl.pallas_call(kernel, out_shape=[jax.ShapeDtypeStruct(s, d) for s, d in...  4.08 us
    all_gather x2, blocking collectives, trade_secs(): even_in = lax.all_gather(even, axes, axis_index_groups=sec_even)  3.68 us
  transfers between devices with their start and end apart: 2, of which 0 were waited for; matrix products, arithmetic and copies ran while one was open for 0% of the time, Pallas kernels for 0%

profile of v3, /device:TPU:320, one launch (start us, length us, event | category | flops | bytes accessed | tf_op | source)
XLA Modules:
  0.0 46.8 jit_solution(3451634744886292860)
XLA Ops:
  0.0 1.6 %shard_map.91 = (f32[16,512]{1,0:T(8,128)S(1)}, f32[16,512]{1,0:T(8,128)S(1)}, f32[16,512]{1,0:T(8,128)S(1)}, s32[16,512]{1,0:T(8,128)S(1)}, f32[2,64,128]{2,1,0:T(8,128)S(1)}, /*index=5*/f32[64,128]{1,0:T(8,128)S(1)}) custom-call(s32[1,3]{1,0:T(1,128)} %r_0_.1, f32[2,64,128]{2,1,0:T(8,128)} %bitcast.35, f32[64,128]{1,0:T(8,128)} %bitcast.36, ...), custom_call_target="tpu_custom_call" | custom-call | tf_op jit(solution)/shard_map/pallas_call | solution.py:263
  1.6 1.9 %all-gather = f32[32,512]{1,0:T(8,128)S(1)} all-gather(f32[16,512]{1,0:T(8,128)S(1)} %get-tuple-element.26), channel_id=2, replica_groups={{0,64},{1,65},{2,66},{3,67},{4,68},{5,69},{6,70},{7,71},{8,72},{9,73},{..., dimensions={0}, use_global_device_ids=true | all-gather | bytes 98304 | tf_op jit(solution)/shard_map/all_gather | solution.py:291
  3.4 7.9 %all-gather.1 = f32[32,512]{1,0:T(8,128)S(1)} all-gather(f32[16,512]{1,0:T(8,128)S(1)} %get-tuple-element.28), channel_id=3, replica_groups={{64,128},{65,129},{66,130},{67,131},{68,132},{69,133},{70,134},{71,135}..., dimensions={0}, use_global_device_ids=true | all-gather | bytes 98304 | tf_op jit(solution)/shard_map/all_gather | solution.py:293
  11.4 8.2 %collective-permute-start = (f32[32,512]{1,0:T(8,128)S(1)}, f32[32,512]{1,0:T(8,128)S(1)}, u32[]{:S(2)}, u32[]{:S(2)}) collective-permute-start(f32[32,512]{1,0:T(8,128)S(1)} %get-tuple-element.32), channel_id=1, source_target_pairs={{1,2},{2,1},{3,4},{4,3},{5,6},{6,5},{7,8},{8,7},{9,10},{10,9},{11,... | collective-permute-start | bytes 196616 | tf_op jit(solution)/shard_map/ppermute | solution.py:287
  19.6 4.9 %all-gather.2 = f32[64,512]{1,0:T(8,128)S(1)} all-gather(f32[32,512]{1,0:T(8,128)S(1)} %get-tuple-element.31), channel_id=4, replica_groups={{0,1},{2,3},{4,5},{6,7},{8,9},{10,11},{12,13},{14,15},{16,17},{18,19},{..., dimensions={0}, use_global_device_ids=true | all-gather | bytes 196608 | tf_op jit(solution)/shard_map/all_gather | solution.py:288
  24.6 0.0 collective-permute-done.odd_tile
  24.6 1.2 %shard_map.93 = (f32[2,64,128]{2,1,0:T(8,128)S(1)}, f32[64,128]{1,0:T(8,128)S(1)}, f32[8,512]{1,0:T(8,128)S(1)}, f32[8,512]{1,0:T(8,128)S(1)}) custom-call(f32[2,32,512]{2,1,0:T(8,128)S(1)} %bitcast.29, f32[32,512]{1,0:T(8,128)S(1)} %collective-permute-done.odd_tile, f32[8,512]{1,0:T(8,128)S(1)} %get-tuple-element.33.mid, ...), custom_call_target="tpu_custom_call" | custom-call | tf_op jit(solution)/shard_map/pallas_call | solution.py:263
  25.8 1.8 %all-gather.3 = f32[16,512]{1,0:T(8,128)S(1)} all-gather(f32[8,512]{1,0:T(8,128)S(1)} %get-tuple-element.37), channel_id=5, replica_groups={{0,64},{1,65},{2,66},{3,67},{4,68},{5,69},{6,70},{7,71},{8,72},{9,73},{..., dimensions={0}, use_global_device_ids=true | all-gather | bytes 49152 | tf_op jit(solution)/shard_map/all_gather | solution.py:291
  27.6 7.7 %all-gather.4 = f32[16,512]{1,0:T(8,128)S(1)} all-gather(f32[8,512]{1,0:T(8,128)S(1)} %get-tuple-element.39), channel_id=6, replica_groups={{64,128},{65,129},{66,130},{67,131},{68,132},{69,133},{70,134},{71,135}..., dimensions={0}, use_global_device_ids=true | all-gather | bytes 49152 | tf_op jit(solution)/shard_map/all_gather | solution.py:293
  35.4 5.4 %collective-permute-start.1 = (f32[24,512]{1,0:T(8,128)S(1)}, f32[24,512]{1,0:T(8,128)S(1)}, u32[]{:S(2)}, u32[]{:S(2)}) collective-permute-start(f32[24,512]{1,0:T(8,128)S(1)} %get-tuple-element.42), channel_id=1, source_target_pairs={{1,2},{2,1},{3,4},{4,3},{5,6},{6,5},{7,8},{8,7},{9,10},{10,9},{11,... | collective-permute-start | bytes 147464 | tf_op jit(solution)/shard_map/ppermute | solution.py:287
  40.8 4.8 %all-gather.5 = f32[48,512]{1,0:T(8,128)S(1)} all-gather(f32[24,512]{1,0:T(8,128)S(1)} %get-tuple-element.41), channel_id=7, replica_groups={{0,1},{2,3},{4,5},{6,7},{8,9},{10,11},{12,13},{14,15},{16,17},{18,19},{..., dimensions={0}, use_global_device_ids=true | all-gather | bytes 147456 | tf_op jit(solution)/shard_map/all_gather | solution.py:288
  45.6 0.0 collective-permute-done.1.odd_tile
  45.6 1.2 %shard_map.95 = f32[2,64,128]{2,1,0:T(8,128)} custom-call(f32[2,24,512]{2,1,0:T(8,128)S(1)} %bitcast.30, f32[24,512]{1,0:T(8,128)S(1)} %collective-permute-done.1.odd_tile, f32[8,512]{1,0:T(8,128)S(1)} %get-tuple-element.43.mid, f32[16,512]{1,0:T(8,128)S(1)} %get-tuple-element.34.own, s32[16,512]{1,0:T(8,128)S(1)} %get-tuple-element.35.ids, ...), custom_call_target="tpu_custom_call" | custom-call | tf_op jit(solution)/shard_map/pallas_call | solution.py:263
  (2 shorter events, 0.1 us)
Async XLA Ops:
  11.4 13.2 %collective-permute-start = (f32[32,512]{1,0:T(8,128)S(1)}, f32[32,512]{1,0:T(8,128)S(1)}, u32[]{:S(2)}, u32[]{:S(2)}) collective-permute-start(f32[32,512]{1,0:T(8,128)S(1)} %get-tuple-element.32), channel_id=1, source_target_pairs={{1,2},{2,1},{3,4},{4,3},{5,6},{6,5},{7,8},{8,7},{9,10},{10,9},{11,... | collective-permute-start | bytes 196616 | tf_op jit(solution)/shard_map/ppermute | solution.py:287
  35.4 10.2 %collective-permute-start.1 = (f32[24,512]{1,0:T(8,128)S(1)}, f32[24,512]{1,0:T(8,128)S(1)}, u32[]{:S(2)}, u32[]{:S(2)}) collective-permute-start(f32[24,512]{1,0:T(8,128)S(1)} %get-tuple-element.42), channel_id=1, source_target_pairs={{1,2},{2,1},{3,4},{4,3},{5,6},{6,5},{7,8},{8,7},{9,10},{10,9},{11,... | collective-permute-start | bytes 147464 | tf_op jit(solution)/shard_map/ppermute | solution.py:287

commit v4 on v3

--- a/solution.py
+++ b/solution.py
@@ -23,32 +23,41 @@
     return place == index
 
 
-def gather(table, lane_hot, block_mask):
+def lane_one_hot(lane):
+    place = lax.broadcasted_iota(jnp.int32, (LANES, LANES), 0).astype(BF16)
+    place = jnp.concatenate([place] * (lane.shape[1] // LANES), axis=1)
+    return jnp.where(place == lane.astype(BF16), jnp.bfloat16(1), jnp.bfloat16(0))
+
+
+def wide_rows(rows):
+    return jnp.concatenate(rows, axis=1)
+
+
+def gather(fields, lane_hot, block_mask):
+    high, low = halves(jnp.concatenate(fields, axis=0))
+    table = jnp.concatenate([high, low], axis=1)
+    picked = jnp.dot(table, jnp.concatenate([lane_hot, lane_hot], axis=0), preferred_element_type=F32)
     blocks = block_mask.shape[0]
-    picked = jnp.dot(table, jnp.concatenate([lane_hot, lane_hot], axis=0), preferred_element_type=F32)
     return [
         jnp.sum(jnp.where(block_mask, picked[i * blocks : (i + 1) * blocks], 0.0), axis=0, keepdims=True)
-        for i in range(picked.shape[0] // blocks)
-    ]
-
-
-def table_of(fields):
-    high, low = halves(jnp.concatenate(fields, axis=0))
-    return jnp.concatenate([high, low], axis=1)
+        for i in range(len(fields))
+    ]
 
 
 def scatter(values, lane_hot, block_hot):
     parts = [halves(v) for v in values]
     left = jnp.concatenate([block_hot * p[k] for k in range(2) for p in parts], axis=0)
-    return lax.dot_general(left, lane_hot, (((1,), (1,)), ((), ())), preferred_element_type=F32)
-
-
-def wide(block):
-    return jnp.concatenate([block[8 * i : 8 * i + 8] for i in range(4)], axis=1)
-
-
-def narrow(rows):
-    return jnp.concatenate([rows[:, LANES * i : LANES * (i + 1)] for i in range(4)], axis=0)
+    total = lax.dot_general(left, lane_hot, (((1,), (1,)), ((), ())), preferred_element_type=F32)
+    return total[: total.shape[0] // 2] + total[total.shape[0] // 2 :]
+
+
+def cut(rows):
+    pieces = [row[:, LANES * i : LANES * (i + 1)] for row in rows for i in range(row.shape[1] // LANES)]
+    return pieces + [jnp.zeros_like(pieces[0])] * ((-len(pieces)) % 8)
+
+
+def slot_row(block, place):
+    return jnp.concatenate([block[4 * place + i : 4 * place + i + 1] for i in range(4)], axis=1)
 
 
 def side_sum(block):
@@ -92,9 +101,7 @@
 
 
 def tile_message(halo, slot_rows):
-    pad = (-len(slot_rows)) % 8
-    rows = [wide(h) for h in halo] + slot_rows + [jnp.zeros_like(slot_rows[0])] * pad
-    return jnp.concatenate(rows, axis=0)
+    return jnp.concatenate(halo + cut(slot_rows), axis=0)
 
 
 def spot():
@@ -115,26 +122,20 @@
     for i in range(2):
         uo[i] = field[i]
     co[...] = stiff
-    table = table_of(field)
     slot = lax.broadcasted_iota(jnp.int32, (1, w.shape[2]), 1)
-    sources, targets, blocks, lanes, pulls = [], [], [], [], []
+    rows = [(srow, scol, g) for g in range(3)] + [(trow, tcol, k) for k in range(3)]
+    blocks = [row[g] * 32 + (col[g] >> 7) for row, col, g in rows]
+    lanes = [col[g] & 127 for row, col, g in rows]
+    got = gather(field, lane_one_hot(wide_rows(lanes)), one_hot(wide_rows(blocks), 64))
+    got = [[v[:, slot.shape[1] * g : slot.shape[1] * (g + 1)] for v in got] for g in range(6)]
+    sources = []
     for g in range(3):
         dest = tile + g - 1
         open_group = (sec < n_sec - 1) & (dest >= 0) & (dest < n_tile)
         limit = jnp.where(open_group, count[0:1, g : g + 1], 0)
         weight = jnp.where(slot < limit, w[g], 0.0)
-        col = scol[g]
-        block, lane = srow[g] * 32 + (col >> 7), col & 127
-        blocks.append(block)
-        lanes.append(lane)
-        got = gather(table, one_hot(lane, LANES).astype(BF16), one_hot(block, 64))
-        sources.append([weight * (got[i] - off[g, i : i + 1]) for i in range(2)] + [weight])
-    for k in range(3):
-        col = tcol[k]
-        block, lane = trow[k] * 32 + (col >> 7), col & 127
-        blocks.append(block)
-        lanes.append(lane)
-        targets.append(gather(table, one_hot(lane, LANES).astype(BF16), one_hot(block, 64)))
+        sources.append([weight * (got[g][i] - off[g, i : i + 1]) for i in range(2)] + [weight])
+    targets = got[3:]
     send_secs(sources, targets, even_msg, odd_msg)
     offsets = [off[g, i : i + 1] for g in range(3) for i in range(2)]
     zero = jnp.zeros_like(offsets[0])
@@ -144,8 +145,8 @@
 
 def send_secs(sources, targets, even_msg, odd_msg):
     size = even_msg.shape[0]
-    source = [r for s in sources for r in s]
-    target = [r for s in targets for r in s]
+    source = cut([r for s in sources for r in s])
+    target = cut([r for s in targets for r in s])
     zero = jnp.zeros_like(source[0])
     source = jnp.concatenate(source + [zero] * (size - len(source)), axis=0)
     target = jnp.concatenate(target + [zero] * (size - len(target)), axis=0)
@@ -163,8 +164,7 @@
     n_src = 3 if first else 2
     source, target = arrivals(even_in, odd_in)
     rows = [
-        [source[n_src * g + i : n_src * g + i + 1] for i in range(n_src)]
-        + [target[2 * g + i : 2 * g + i + 1] for i in range(2)]
+        [slot_row(source, n_src * g + i) for i in range(n_src)] + [slot_row(target, 2 * g + i) for i in range(2)]
         for g in range(3)
     ]
     stiff = c[...]
@@ -176,19 +176,20 @@
 
 
 def slot_arrivals(first, even_in, odd_in, mid):
-    base = 24 if first else 16
+    base = 96 if first else 64
     n_src = 3 if first else 2
-    left, right = both_sides(even_in, odd_in, slice(base, base + 8))
-    sides = (left, mid[...], right)
-    source = [m[i : i + 1] for m in sides for i in range(n_src)]
-    target = [m[n_src + i : n_src + i + 1] for m in sides for i in range(2)]
+    left, right = both_sides(even_in, odd_in, slice(base, even_in.shape[1]))
+    sides = [[slot_row(m, i) for i in range(n_src + 2)] for m in (left, right)]
+    sides.insert(1, [mid[i : i + 1, :] for i in range(n_src + 2)])
+    source = [m[i] for m in sides for i in range(n_src)]
+    target = [m[n_src + i] for m in sides for i in range(2)]
     return source, target
 
 
 def springs(fields, even_in, odd_in):
-    up, down = both_sides(even_in, odd_in, slice(0, 8 * len(fields)))
+    up, down = both_sides(even_in, odd_in, slice(0, 32 * len(fields)))
     return [
-        stencil(narrow(up[8 * i : 8 * i + 8]), f[:32], f[32:], narrow(down[8 * i : 8 * i + 8]))
+        stencil(up[32 * i : 32 * i + 32], f[:32], f[32:], down[32 * i : 32 * i + 32])
         for i, f in enumerate(fields)
     ]
 
@@ -206,24 +207,22 @@
 
 
 def hots_of(ids):
-    return [(one_hot(ids[6 + g : 7 + g], LANES).astype(BF16), one_hot(ids[g : g + 1], 64)) for g in range(6)]
-
-
-def middle_kernel(
-    even_tile, odd_tile, mid, own, ids, u, c, u_out, total_out, even_msg, odd_msg
-):
+    lane = wide_rows([ids[6 + g : 7 + g] for g in range(6)])
+    block = wide_rows([ids[g : g + 1] for g in range(6)])
+    return lane_one_hot(lane), one_hot(block, 64)
+
+
+def middle_kernel(even_tile, odd_tile, mid, own, ids, u, c, u_out, total_out, even_msg, odd_msg):
     source_in, target_in = slot_arrivals(True, even_tile, odd_tile, mid)
     off = offset_rows(own)
-    hots = hots_of(ids[...])
+    lane_hot, block_mask = hots_of(ids[...])
     weights = [own[5 + g : 6 + g, :] for g in range(3)]
-    acc = jnp.zeros((384, LANES), F32)
-    for g in range(6):
-        if g < 3:
-            vals = [weights[g] * (target_in[2 * g + i] + off(g, i)) for i in range(2)] + [weights[g]]
-        else:
-            vals = [source_in[3 * (g - 3) + i] for i in range(3)]
-        acc = acc + scatter(vals, hots[g][0], hots[g][1].astype(BF16))
-    acc = acc[:192] + acc[192:]
+    values = [
+        wide_rows([weights[g] * (target_in[2 * g + i] + off(g, i)) for g in range(3)] + [source_in[3 * k + i] for k in range(3)])
+        for i in range(2)
+    ]
+    values.append(wide_rows(weights + [source_in[3 * k + 2] for k in range(3)]))
+    acc = scatter(values, lane_hot, block_mask.astype(BF16))
     stiff = c[...]
     near = springs([stiff * u[0], stiff * u[1], stiff], even_tile, odd_tile)
     share = damping / (stiff * near[2] + acc[128:192])
@@ -231,8 +230,9 @@
     field = [(1.0 - damping) * u[i] + (stiff * near[i] + acc[64 * i : 64 * i + 64]) * share for i in range(2)]
     for i in range(2):
         u_out[i] = field[i]
-    table = table_of(field)
-    got = [gather(table, *h) for h in hots]
+    got = gather(field, lane_hot, block_mask)
+    size = weights[0].shape[1]
+    got = [[v[:, size * g : size * (g + 1)] for v in got] for g in range(6)]
     sources = [[weights[g] * (got[g][i] - off(g, i)) for i in range(2)] for g in range(3)]
     send_secs(sources, got[3:], even_msg, odd_msg)
 
@@ -240,16 +240,13 @@
 def last_kernel(even_tile, odd_tile, mid, own, ids, u, c, share, out):
     source_in, target_in = slot_arrivals(False, even_tile, odd_tile, mid)
     off = offset_rows(own)
-    hots = hots_of(ids[...])
-    acc = jnp.zeros((256, LANES), F32)
-    for g in range(6):
-        if g < 3:
-            weight = own[5 + g : 6 + g, :]
-            vals = [weight * (target_in[2 * g + i] + off(g, i)) for i in range(2)]
-        else:
-            vals = [source_in[2 * (g - 3) + i] for i in range(2)]
-        acc = acc + scatter(vals, hots[g][0], hots[g][1].astype(BF16))
-    acc = acc[:128] + acc[128:]
+    lane_hot, block_mask = hots_of(ids[...])
+    weights = [own[5 + g : 6 + g, :] for g in range(3)]
+    values = [
+        wide_rows([weights[g] * (target_in[2 * g + i] + off(g, i)) for g in range(3)] + [source_in[2 * k + i] for k in range(3)])
+        for i in range(2)
+    ]
+    acc = scatter(values, lane_hot, block_mask.astype(BF16))
     stiff = c[...]
     near = springs([stiff * u[0], stiff * u[1]], even_tile, odd_tile)
     for i in range(2):
@@ -298,20 +295,20 @@
     off = match_offset[0].transpose(1, 0, 2)
     even, odd, own, ids, u, c = call(
         lambda *r: first_kernel(n_sec, n_tile, *r),
-        [((16, slots), F32), ((16, slots), F32), ((16, slots), F32), ((16, slots), jnp.int32), ((2, 64, LANES), F32), ((64, LANES), F32)],
+        [((40, LANES), F32), ((40, LANES), F32), ((16, slots), F32), ((16, slots), jnp.int32), ((2, 64, LANES), F32), ((64, LANES), F32)],
         match_count, u, c, w, off, srow, scol, trow, tcol,
         held=True,
     )
     even, odd, mid = call(
-        lambda *r: pack_kernel(True, *r), [((32, slots), F32)] * 2 + [((8, slots), F32)], *trade_secs(even, odd), u, c
+        lambda *r: pack_kernel(True, *r), [((120, LANES), F32)] * 2 + [((8, slots), F32)], *trade_secs(even, odd), u, c
     )
     u, share, even, odd = call(
         middle_kernel,
-        [((2, 64, LANES), F32), ((64, LANES), F32), ((8, slots), F32), ((8, slots), F32)],
+        [((2, 64, LANES), F32), ((64, LANES), F32), ((24, LANES), F32), ((24, LANES), F32)],
         *trade_tiles(even, odd), mid, own, ids, u, c,
     )
     even, odd, mid = call(
-        lambda *r: pack_kernel(False, *r), [((24, slots), F32)] * 2 + [((8, slots), F32)], *trade_secs(even, odd), u, c
+        lambda *r: pack_kernel(False, *r), [((80, LANES), F32)] * 2 + [((8, slots), F32)], *trade_secs(even, odd), u, c
     )
     (out,) = call(last_kernel, [((2, 64, LANES), F32)], *trade_tiles(even, odd), mid, own, ids, u, c, share)
     return out.reshape(2, 32, 2, LANES).transpose(0, 2, 1, 3).reshape(1, 2, 2, 32 * LANES)

time: 47.1 us -> 46.1 us (0.979)
  starting transfers between devices: 13.7 us -> 13.2 us
    ppermute x2, starting transfers between devices: 13.7 us -> 13.2 us  [trade_tiles(): lax.ppermute(odd, axes, [q for a, b in tile_odd for q in ((a, b), (b, a))])]
where the time goes in v4:
time: 46.1 us; the launch traced here: 45.9 us
  blocking collectives  28.7 us (62%)
  starting transfers between devices  13.2 us (29%)
  Pallas kernels  3.94 us (9%)
    all_gather x2, blocking collectives, trade_secs(): return (even_in, lax.all_gather(odd, axes, axis_index_groups=sec_odd))  15.5 us
    ppermute x2, starting transfers between devices, trade_tiles(): lax.ppermute(odd, axes, [q for a, b in tile_odd for q in ((a, b), (b, a))])  13.2 us
    all_gather x2, blocking collectives, trade_tiles(): return (lax.all_gather(even, axes, axis_index_groups=tile_even), swapped)  9.58 us
    pallas_call x5, Pallas kernels, call(): pl.pallas_call(kernel, out_shape=[jax.ShapeDtypeStruct(s, d) for s, d in...  3.94 us
    all_gather x2, blocking collectives, trade_secs(): even_in = lax.all_gather(even, axes, axis_index_groups=sec_even)  3.66 us
  transfers between devices with their start and end apart: 2, of which 0 were waited for; matrix products, arithmetic and copies ran while one was open for 0% of the time, Pallas kernels for 0%

profile of v4, /device:TPU:320, one launch (start us, length us, event | category | flops | bytes accessed | tf_op | source)
XLA Modules:
  0.0 45.9 jit_solution(15225985607535553198)
XLA Ops:
  0.0 1.4 %shard_map.91 = (f32[40,128]{1,0:T(8,128)S(1)}, f32[40,128]{1,0:T(8,128)S(1)}, f32[16,512]{1,0:T(8,128)S(1)}, s32[16,512]{1,0:T(8,128)S(1)}, f32[2,64,128]{2,1,0:T(8,128)S(1)}, /*index=5*/f32[64,128]{1,0:T(8,128)S(1)}) custom-call(s32[1,3]{1,0:T(1,128)} %r_0_.1, f32[2,64,128]{2,1,0:T(8,128)} %bitcast.35, f32[64,128]{1,0:T(8,128)} %bitcast.36, ...), custom_call_target="tpu_custom_call" | custom-call | tf_op jit(solution)/shard_map/pallas_call | solution.py:260
  1.4 1.8 %all-gather = f32[80,128]{1,0:T(8,128)S(1)} all-gather(f32[40,128]{1,0:T(8,128)S(1)} %get-tuple-element.26), channel_id=2, replica_groups={{0,64},{1,65},{2,66},{3,67},{4,68},{5,69},{6,70},{7,71},{8,72},{9,73},{..., dimensions={0}, use_global_device_ids=true | all-gather | bytes 61440 | tf_op jit(solution)/shard_map/all_gather | solution.py:288
  3.3 7.8 %all-gather.1 = f32[80,128]{1,0:T(8,128)S(1)} all-gather(f32[40,128]{1,0:T(8,128)S(1)} %get-tuple-element.28), channel_id=3, replica_groups={{64,128},{65,129},{66,130},{67,131},{68,132},{69,133},{70,134},{71,135}..., dimensions={0}, use_global_device_ids=true | all-gather | bytes 61440 | tf_op jit(solution)/shard_map/all_gather | solution.py:290
  11.1 7.8 %collective-permute-start = (f32[120,128]{1,0:T(8,128)S(1)}, f32[120,128]{1,0:T(8,128)S(1)}, u32[]{:S(2)}, u32[]{:S(2)}) collective-permute-start(f32[120,128]{1,0:T(8,128)S(1)} %get-tuple-element.32), channel_id=1, source_target_pairs={{1,2},{2,1},{3,4},{4,3},{5,6},{6,5},{7,8},{8,7},{9,10},{10,9},{11,... | collective-permute-start | bytes 184328 | tf_op jit(solution)/shard_map/ppermute | solution.py:284
  18.9 4.9 %all-gather.2 = f32[240,128]{1,0:T(8,128)S(1)} all-gather(f32[120,128]{1,0:T(8,128)S(1)} %get-tuple-element.31), channel_id=4, replica_groups={{0,1},{2,3},{4,5},{6,7},{8,9},{10,11},{12,13},{14,15},{16,17},{18,19},{..., dimensions={0}, use_global_device_ids=true | all-gather | bytes 184320 | tf_op jit(solution)/shard_map/all_gather | solution.py:285
  23.8 0.0 collective-permute-done.odd_tile
  23.8 1.2 %shard_map.93 = (f32[2,64,128]{2,1,0:T(8,128)S(1)}, f32[64,128]{1,0:T(8,128)S(1)}, f32[24,128]{1,0:T(8,128)S(1)}, f32[24,128]{1,0:T(8,128)S(1)}) custom-call(f32[2,120,128]{2,1,0:T(8,128)S(1)} %bitcast.29, f32[120,128]{1,0:T(8,128)S(1)} %collective-permute-done.odd_tile, f32[8,512]{1,0:T(8,128)S(1)} %get-tuple-element.33.mid, ...), custom_call_target="tpu_custom_call" | custom-call | tf_op jit(solution)/shard_map/pallas_call | solution.py:260
  25.0 1.8 %all-gather.3 = f32[48,128]{1,0:T(8,128)S(1)} all-gather(f32[24,128]{1,0:T(8,128)S(1)} %get-tuple-element.37), channel_id=5, replica_groups={{0,64},{1,65},{2,66},{3,67},{4,68},{5,69},{6,70},{7,71},{8,72},{9,73},{..., dimensions={0}, use_global_device_ids=true | all-gather | bytes 36864 | tf_op jit(solution)/shard_map/all_gather | solution.py:288
  26.8 7.7 %all-gather.4 = f32[48,128]{1,0:T(8,128)S(1)} all-gather(f32[24,128]{1,0:T(8,128)S(1)} %get-tuple-element.39), channel_id=6, replica_groups={{64,128},{65,129},{66,130},{67,131},{68,132},{69,133},{70,134},{71,135}..., dimensions={0}, use_global_device_ids=true | all-gather | bytes 36864 | tf_op jit(solution)/shard_map/all_gather | solution.py:290
  34.6 5.4 %collective-permute-start.1 = (f32[80,128]{1,0:T(8,128)S(1)}, f32[80,128]{1,0:T(8,128)S(1)}, u32[]{:S(2)}, u32[]{:S(2)}) collective-permute-start(f32[80,128]{1,0:T(8,128)S(1)} %get-tuple-element.42), channel_id=1, source_target_pairs={{1,2},{2,1},{3,4},{4,3},{5,6},{6,5},{7,8},{8,7},{9,10},{10,9},{11,... | collective-permute-start | bytes 122888 | tf_op jit(solution)/shard_map/ppermute | solution.py:284
  40.0 4.7 %all-gather.5 = f32[160,128]{1,0:T(8,128)S(1)} all-gather(f32[80,128]{1,0:T(8,128)S(1)} %get-tuple-element.41), channel_id=7, replica_groups={{0,1},{2,3},{4,5},{6,7},{8,9},{10,11},{12,13},{14,15},{16,17},{18,19},{..., dimensions={0}, use_global_device_ids=true | all-gather | bytes 122880 | tf_op jit(solution)/shard_map/all_gather | solution.py:285
  44.7 0.0 collective-permute-done.1.odd_tile
  44.7 1.2 %shard_map.95 = f32[2,64,128]{2,1,0:T(8,128)} custom-call(f32[2,80,128]{2,1,0:T(8,128)S(1)} %bitcast.30, f32[80,128]{1,0:T(8,128)S(1)} %collective-permute-done.1.odd_tile, f32[8,512]{1,0:T(8,128)S(1)} %get-tuple-element.43.mid, f32[16,512]{1,0:T(8,128)S(1)} %get-tuple-element.34.own, s32[16,512]{1,0:T(8,128)S(1)} %get-tuple-element.35.ids, ...), custom_call_target="tpu_custom_call" | custom-call | tf_op jit(solution)/shard_map/pallas_call | solution.py:260
  (2 shorter events, 0.1 us)
Async XLA Ops:
  11.1 12.7 %collective-permute-start = (f32[120,128]{1,0:T(8,128)S(1)}, f32[120,128]{1,0:T(8,128)S(1)}, u32[]{:S(2)}, u32[]{:S(2)}) collective-permute-start(f32[120,128]{1,0:T(8,128)S(1)} %get-tuple-element.32), channel_id=1, source_target_pairs={{1,2},{2,1},{3,4},{4,3},{5,6},{6,5},{7,8},{8,7},{9,10},{10,9},{11,... | collective-permute-start | bytes 184328 | tf_op jit(solution)/shard_map/ppermute | solution.py:284
  34.6 10.1 %collective-permute-start.1 = (f32[80,128]{1,0:T(8,128)S(1)}, f32[80,128]{1,0:T(8,128)S(1)}, u32[]{:S(2)}, u32[]{:S(2)}) collective-permute-start(f32[80,128]{1,0:T(8,128)S(1)} %get-tuple-element.42), channel_id=1, source_target_pairs={{1,2},{2,1},{3,4},{4,3},{5,6},{6,5},{7,8},{8,7},{9,10},{10,9},{11,... | collective-permute-start | bytes 122888 | tf_op jit(solution)/shard_map/ppermute | solution.py:284

commit v5 on v4

--- a/solution.py
+++ b/solution.py
@@ -45,10 +45,8 @@
 
 
 def scatter(values, lane_hot, block_hot):
-    parts = [halves(v) for v in values]
-    left = jnp.concatenate([block_hot * p[k] for k in range(2) for p in parts], axis=0)
-    total = lax.dot_general(left, lane_hot, (((1,), (1,)), ((), ())), preferred_element_type=F32)
-    return total[: total.shape[0] // 2] + total[total.shape[0] // 2 :]
+    left = jnp.concatenate([block_hot * v.astype(BF16) for v in values], axis=0)
+    return lax.dot_general(left, lane_hot, (((1,), (1,)), ((), ())), preferred_element_type=F32)
 
 
 def cut(rows):

time: 46.1 us -> 45.7 us (level)
  Pallas kernels: 3.94 us -> 3.45 us
    pallas_call x5, Pallas kernels: 3.94 us -> 3.45 us  [call(): pl.pallas_call(kernel, out_shape=[jax.ShapeDtypeStruct(s, d) for s, d in...]
where the time goes in v5:
time: 45.7 us; the launch traced here: 45.4 us
  blocking collectives  28.7 us (63%)
  starting transfers between devices  13.2 us (29%)
  Pallas kernels  3.45 us (8%)
    all_gather x2, blocking collectives, trade_secs(): return (even_in, lax.all_gather(odd, axes, axis_index_groups=sec_odd))  15.5 us
    ppermute x2, starting transfers between devices, trade_tiles(): lax.ppermute(odd, axes, [q for a, b in tile_odd for q in ((a, b), (b, a))])  13.2 us
    all_gather x2, blocking collectives, trade_tiles(): return (lax.all_gather(even, axes, axis_index_groups=tile_even), swapped)  9.58 us
    all_gather x2, blocking collectives, trade_secs(): even_in = lax.all_gather(even, axes, axis_index_groups=sec_even)  3.66 us
    pallas_call x5, Pallas kernels, call(): pl.pallas_call(kernel, out_shape=[jax.ShapeDtypeStruct(s, d) for s, d in...  3.45 us
  transfers between devices with their start and end apart: 2, of which 0 were waited for; matrix products, arithmetic and copies ran while one was open for 0% of the time, Pallas kernels for 0%

profile of v5, /device:TPU:320, one launch (start us, length us, event | category | flops | bytes accessed | tf_op | source)
XLA Modules:
  0.0 45.4 jit_solution(7972171256925214158)
XLA Ops:
  0.0 1.4 %shard_map.91 = (f32[40,128]{1,0:T(8,128)S(1)}, f32[40,128]{1,0:T(8,128)S(1)}, f32[16,512]{1,0:T(8,128)S(1)}, s32[16,512]{1,0:T(8,128)S(1)}, f32[2,64,128]{2,1,0:T(8,128)S(1)}, /*index=5*/f32[64,128]{1,0:T(8,128)S(1)}) custom-call(s32[1,3]{1,0:T(1,128)} %r_0_.1, f32[2,64,128]{2,1,0:T(8,128)} %bitcast.35, f32[64,128]{1,0:T(8,128)} %bitcast.36, ...), custom_call_target="tpu_custom_call" | custom-call | tf_op jit(solution)/shard_map/pallas_call | solution.py:258
  1.4 1.8 %all-gather = f32[80,128]{1,0:T(8,128)S(1)} all-gather(f32[40,128]{1,0:T(8,128)S(1)} %get-tuple-element.26), channel_id=2, replica_groups={{0,64},{1,65},{2,66},{3,67},{4,68},{5,69},{6,70},{7,71},{8,72},{9,73},{..., dimensions={0}, use_global_device_ids=true | all-gather | bytes 61440 | tf_op jit(solution)/shard_map/all_gather | solution.py:286
  3.3 7.8 %all-gather.1 = f32[80,128]{1,0:T(8,128)S(1)} all-gather(f32[40,128]{1,0:T(8,128)S(1)} %get-tuple-element.28), channel_id=3, replica_groups={{64,128},{65,129},{66,130},{67,131},{68,132},{69,133},{70,134},{71,135}..., dimensions={0}, use_global_device_ids=true | all-gather | bytes 61440 | tf_op jit(solution)/shard_map/all_gather | solution.py:288
  11.1 7.8 %collective-permute-start = (f32[120,128]{1,0:T(8,128)S(1)}, f32[120,128]{1,0:T(8,128)S(1)}, u32[]{:S(2)}, u32[]{:S(2)}) collective-permute-start(f32[120,128]{1,0:T(8,128)S(1)} %get-tuple-element.32), channel_id=1, source_target_pairs={{1,2},{2,1},{3,4},{4,3},{5,6},{6,5},{7,8},{8,7},{9,10},{10,9},{11,... | collective-permute-start | bytes 184328 | tf_op jit(solution)/shard_map/ppermute | solution.py:282
  18.9 4.9 %all-gather.2 = f32[240,128]{1,0:T(8,128)S(1)} all-gather(f32[120,128]{1,0:T(8,128)S(1)} %get-tuple-element.31), channel_id=4, replica_groups={{0,1},{2,3},{4,5},{6,7},{8,9},{10,11},{12,13},{14,15},{16,17},{18,19},{..., dimensions={0}, use_global_device_ids=true | all-gather | bytes 184320 | tf_op jit(solution)/shard_map/all_gather | solution.py:283
  23.8 0.0 collective-permute-done.odd_tile
  23.8 0.9 %shard_map.93 = (f32[2,64,128]{2,1,0:T(8,128)S(1)}, f32[64,128]{1,0:T(8,128)S(1)}, f32[24,128]{1,0:T(8,128)S(1)}, f32[24,128]{1,0:T(8,128)S(1)}) custom-call(f32[2,120,128]{2,1,0:T(8,128)S(1)} %bitcast.29, f32[120,128]{1,0:T(8,128)S(1)} %collective-permute-done.odd_tile, f32[8,512]{1,0:T(8,128)S(1)} %get-tuple-element.33.mid, ...), custom_call_target="tpu_custom_call" | custom-call | tf_op jit(solution)/shard_map/pallas_call | solution.py:258
  24.7 1.8 %all-gather.3 = f32[48,128]{1,0:T(8,128)S(1)} all-gather(f32[24,128]{1,0:T(8,128)S(1)} %get-tuple-element.37), channel_id=5, replica_groups={{0,64},{1,65},{2,66},{3,67},{4,68},{5,69},{6,70},{7,71},{8,72},{9,73},{..., dimensions={0}, use_global_device_ids=true | all-gather | bytes 36864 | tf_op jit(solution)/shard_map/all_gather | solution.py:286
  26.5 7.7 %all-gather.4 = f32[48,128]{1,0:T(8,128)S(1)} all-gather(f32[24,128]{1,0:T(8,128)S(1)} %get-tuple-element.39), channel_id=6, replica_groups={{64,128},{65,129},{66,130},{67,131},{68,132},{69,133},{70,134},{71,135}..., dimensions={0}, use_global_device_ids=true | all-gather | bytes 36864 | tf_op jit(solution)/shard_map/all_gather | solution.py:288
  34.3 5.4 %collective-permute-start.1 = (f32[80,128]{1,0:T(8,128)S(1)}, f32[80,128]{1,0:T(8,128)S(1)}, u32[]{:S(2)}, u32[]{:S(2)}) collective-permute-start(f32[80,128]{1,0:T(8,128)S(1)} %get-tuple-element.42), channel_id=1, source_target_pairs={{1,2},{2,1},{3,4},{4,3},{5,6},{6,5},{7,8},{8,7},{9,10},{10,9},{11,... | collective-permute-start | bytes 122888 | tf_op jit(solution)/shard_map/ppermute | solution.py:282
  39.7 4.7 %all-gather.5 = f32[160,128]{1,0:T(8,128)S(1)} all-gather(f32[80,128]{1,0:T(8,128)S(1)} %get-tuple-element.41), channel_id=7, replica_groups={{0,1},{2,3},{4,5},{6,7},{8,9},{10,11},{12,13},{14,15},{16,17},{18,19},{..., dimensions={0}, use_global_device_ids=true | all-gather | bytes 122880 | tf_op jit(solution)/shard_map/all_gather | solution.py:283
  44.4 0.0 collective-permute-done.1.odd_tile
  44.4 1.0 %shard_map.95 = f32[2,64,128]{2,1,0:T(8,128)} custom-call(f32[2,80,128]{2,1,0:T(8,128)S(1)} %bitcast.30, f32[80,128]{1,0:T(8,128)S(1)} %collective-permute-done.1.odd_tile, f32[8,512]{1,0:T(8,128)S(1)} %get-tuple-element.43.mid, f32[16,512]{1,0:T(8,128)S(1)} %get-tuple-element.34.own, s32[16,512]{1,0:T(8,128)S(1)} %get-tuple-element.35.ids, ...), custom_call_target="tpu_custom_call" | custom-call | tf_op jit(solution)/shard_map/pallas_call | solution.py:258
  (2 shorter events, 0.1 us)
Async XLA Ops:
  11.1 12.7 %collective-permute-start = (f32[120,128]{1,0:T(8,128)S(1)}, f32[120,128]{1,0:T(8,128)S(1)}, u32[]{:S(2)}, u32[]{:S(2)}) collective-permute-start(f32[120,128]{1,0:T(8,128)S(1)} %get-tuple-element.32), channel_id=1, source_target_pairs={{1,2},{2,1},{3,4},{4,3},{5,6},{6,5},{7,8},{8,7},{9,10},{10,9},{11,... | collective-permute-start | bytes 184328 | tf_op jit(solution)/shard_map/ppermute | solution.py:282
  34.3 10.1 %collective-permute-start.1 = (f32[80,128]{1,0:T(8,128)S(1)}, f32[80,128]{1,0:T(8,128)S(1)}, u32[]{:S(2)}, u32[]{:S(2)}) collective-permute-start(f32[80,128]{1,0:T(8,128)S(1)} %get-tuple-element.42), channel_id=1, source_target_pairs={{1,2},{2,1},{3,4},{4,3},{5,6},{6,5},{7,8},{8,7},{9,10},{10,9},{11,... | collective-permute-start | bytes 122888 | tf_op jit(solution)/shard_map/ppermute | solution.py:282

commit v6 on v5

--- a/solution.py
+++ b/solution.py
@@ -23,8 +23,8 @@
     return place == index
 
 
-def lane_one_hot(lane):
-    place = lax.broadcasted_iota(jnp.int32, (LANES, LANES), 0).astype(BF16)
+def lane_one_hot(lane, depth=LANES):
+    place = lax.broadcasted_iota(jnp.int32, (depth, LANES), 0).astype(BF16)
     place = jnp.concatenate([place] * (lane.shape[1] // LANES), axis=1)
     return jnp.where(place == lane.astype(BF16), jnp.bfloat16(1), jnp.bfloat16(0))
 
@@ -40,6 +40,16 @@
     blocks = block_mask.shape[0]
     return [
         jnp.sum(jnp.where(block_mask, picked[i * blocks : (i + 1) * blocks], 0.0), axis=0, keepdims=True)
+        for i in range(len(fields))
+    ]
+
+
+def gather_rows(fields, lane_hot, block_mask):
+    high, low = halves(jnp.concatenate([jnp.concatenate([f[:32], f[32:]], axis=1) for f in fields], axis=0))
+    picked = jnp.dot(jnp.concatenate([high, low], axis=0), lane_hot, preferred_element_type=F32)
+    picked = picked[: high.shape[0]] + picked[high.shape[0] :]
+    return [
+        jnp.sum(jnp.where(block_mask, picked[32 * i : 32 * i + 32], 0.0), axis=0, keepdims=True)
         for i in range(len(fields))
     ]
 
@@ -111,20 +121,24 @@
     copies = [pltpu.make_async_copy(f, h, sems.at[i]) for i, (f, h) in enumerate(zip(far, held))]
     for copy in copies:
         copy.start()
-    for copy in copies:
+    srow, scol, trow, tcol, u, c, w, off, count = held
+    for copy in copies[:4]:
         copy.wait()
-    count, u, c, w, off, srow, scol, trow, tcol = held
     sec, tile = spot()
+    rows = [(srow[g], scol[g]) for g in range(3)] + [(trow[k], tcol[k]) for k in range(3)]
+    blocks = [row * 32 + (col >> 7) for row, col in rows]
+    lanes = [col & 127 for row, col in rows]
+    lane_hot = lane_one_hot(wide_rows([row * LANES + (col & 127) for row, col in rows]), 2 * LANES)
+    block_mask = one_hot(wide_rows([col >> 7 for row, col in rows]), 32)
+    for copy in copies[4:]:
+        copy.wait()
     field = [jnp.concatenate(rows_of(u, (i,)), axis=0) for i in range(2)]
     stiff = jnp.concatenate(rows_of(c), axis=0)
     for i in range(2):
         uo[i] = field[i]
     co[...] = stiff
     slot = lax.broadcasted_iota(jnp.int32, (1, w.shape[2]), 1)
-    rows = [(srow, scol, g) for g in range(3)] + [(trow, tcol, k) for k in range(3)]
-    blocks = [row[g] * 32 + (col[g] >> 7) for row, col, g in rows]
-    lanes = [col[g] & 127 for row, col, g in rows]
-    got = gather(field, lane_one_hot(wide_rows(lanes)), one_hot(wide_rows(blocks), 64))
+    got = gather_rows(field, lane_hot, block_mask)
     got = [[v[:, slot.shape[1] * g : slot.shape[1] * (g + 1)] for v in got] for g in range(6)]
     sources = []
     for g in range(3):
@@ -294,7 +308,7 @@
     even, odd, own, ids, u, c = call(
         lambda *r: first_kernel(n_sec, n_tile, *r),
         [((40, LANES), F32), ((40, LANES), F32), ((16, slots), F32), ((16, slots), jnp.int32), ((2, 64, LANES), F32), ((64, LANES), F32)],
-        match_count, u, c, w, off, srow, scol, trow, tcol,
+        srow, scol, trow, tcol, u, c, w, off, match_count,
         held=True,
     )
     even, odd, mid = call(

time: 45.7 us -> 45.6 us (level)
  no operation moved by 1% of the time
where the time goes in v6:
time: 45.6 us; the launch traced here: 45.4 us
  blocking collectives  28.7 us (63%)
  starting transfers between devices  13.2 us (29%)
  Pallas kernels  3.43 us (8%)
    all_gather x2, blocking collectives, trade_secs(): return (even_in, lax.all_gather(odd, axes, axis_index_groups=sec_odd))  15.5 us
    ppermute x2, starting transfers between devices, trade_tiles(): lax.ppermute(odd, axes, [q for a, b in tile_odd for q in ((a, b), (b, a))])  13.2 us
    all_gather x2, blocking collectives, trade_tiles(): return (lax.all_gather(even, axes, axis_index_groups=tile_even), swapped)  9.58 us
    all_gather x2, blocking collectives, trade_secs(): even_in = lax.all_gather(even, axes, axis_index_groups=sec_even)  3.66 us
    pallas_call x5, Pallas kernels, call(): pl.pallas_call(kernel, out_shape=[jax.ShapeDtypeStruct(s, d) for s, d in...  3.43 us
  transfers between devices with their start and end apart: 2, of which 0 were waited for; matrix products, arithmetic and copies ran while one was open for 0% of the time, Pallas kernels for 0%

profile of v6, /device:TPU:320, one launch (start us, length us, event | category | flops | bytes accessed | tf_op | source)
XLA Modules:
  0.0 45.4 jit_solution(4778230573591161976)
XLA Ops:
  0.0 1.4 %shard_map.91 = (f32[40,128]{1,0:T(8,128)S(1)}, f32[40,128]{1,0:T(8,128)S(1)}, f32[16,512]{1,0:T(8,128)S(1)}, s32[16,512]{1,0:T(8,128)S(1)}, f32[2,64,128]{2,1,0:T(8,128)S(1)}, /*index=5*/f32[64,128]{1,0:T(8,128)S(1)}) custom-call(s32[3,1,512]{2,1,0:T(1,128)} %bitcast.38, s32[3,1,512]{2,1,0:T(1,128)} %bitcast.39, s32[3,1,512]{2,1,0:T(1,128)} %bitcast.40, ...), custom_call_target="tpu_custom_call" | custom-call | tf_op jit(solution)/shard_map/pallas_call | solution.py:272
  1.4 1.8 %all-gather = f32[80,128]{1,0:T(8,128)S(1)} all-gather(f32[40,128]{1,0:T(8,128)S(1)} %get-tuple-element.26), channel_id=2, replica_groups={{0,64},{1,65},{2,66},{3,67},{4,68},{5,69},{6,70},{7,71},{8,72},{9,73},{..., dimensions={0}, use_global_device_ids=true | all-gather | bytes 61440 | tf_op jit(solution)/shard_map/all_gather | solution.py:300
  3.2 7.8 %all-gather.1 = f32[80,128]{1,0:T(8,128)S(1)} all-gather(f32[40,128]{1,0:T(8,128)S(1)} %get-tuple-element.28), channel_id=3, replica_groups={{64,128},{65,129},{66,130},{67,131},{68,132},{69,133},{70,134},{71,135}..., dimensions={0}, use_global_device_ids=true | all-gather | bytes 61440 | tf_op jit(solution)/shard_map/all_gather | solution.py:302
  11.1 7.8 %collective-permute-start = (f32[120,128]{1,0:T(8,128)S(1)}, f32[120,128]{1,0:T(8,128)S(1)}, u32[]{:S(2)}, u32[]{:S(2)}) collective-permute-start(f32[120,128]{1,0:T(8,128)S(1)} %get-tuple-element.32), channel_id=1, source_target_pairs={{1,2},{2,1},{3,4},{4,3},{5,6},{6,5},{7,8},{8,7},{9,10},{10,9},{11,... | collective-permute-start | bytes 184328 | tf_op jit(solution)/shard_map/ppermute | solution.py:296
  18.8 4.9 %all-gather.2 = f32[240,128]{1,0:T(8,128)S(1)} all-gather(f32[120,128]{1,0:T(8,128)S(1)} %get-tuple-element.31), channel_id=4, replica_groups={{0,1},{2,3},{4,5},{6,7},{8,9},{10,11},{12,13},{14,15},{16,17},{18,19},{..., dimensions={0}, use_global_device_ids=true | all-gather | bytes 184320 | tf_op jit(solution)/shard_map/all_gather | solution.py:297
  23.7 0.0 collective-permute-done.odd_tile
  23.7 0.9 %shard_map.93 = (f32[2,64,128]{2,1,0:T(8,128)S(1)}, f32[64,128]{1,0:T(8,128)S(1)}, f32[24,128]{1,0:T(8,128)S(1)}, f32[24,128]{1,0:T(8,128)S(1)}) custom-call(f32[2,120,128]{2,1,0:T(8,128)S(1)} %bitcast.29, f32[120,128]{1,0:T(8,128)S(1)} %collective-permute-done.odd_tile, f32[8,512]{1,0:T(8,128)S(1)} %get-tuple-element.33.mid, ...), custom_call_target="tpu_custom_call" | custom-call | tf_op jit(solution)/shard_map/pallas_call | solution.py:272
  24.7 1.8 %all-gather.3 = f32[48,128]{1,0:T(8,128)S(1)} all-gather(f32[24,128]{1,0:T(8,128)S(1)} %get-tuple-element.37), channel_id=5, replica_groups={{0,64},{1,65},{2,66},{3,67},{4,68},{5,69},{6,70},{7,71},{8,72},{9,73},{..., dimensions={0}, use_global_device_ids=true | all-gather | bytes 36864 | tf_op jit(solution)/shard_map/all_gather | solution.py:300
  26.5 7.7 %all-gather.4 = f32[48,128]{1,0:T(8,128)S(1)} all-gather(f32[24,128]{1,0:T(8,128)S(1)} %get-tuple-element.39), channel_id=6, replica_groups={{64,128},{65,129},{66,130},{67,131},{68,132},{69,133},{70,134},{71,135}..., dimensions={0}, use_global_device_ids=true | all-gather | bytes 36864 | tf_op jit(solution)/shard_map/all_gather | solution.py:302
  34.3 5.4 %collective-permute-start.1 = (f32[80,128]{1,0:T(8,128)S(1)}, f32[80,128]{1,0:T(8,128)S(1)}, u32[]{:S(2)}, u32[]{:S(2)}) collective-permute-start(f32[80,128]{1,0:T(8,128)S(1)} %get-tuple-element.42), channel_id=1, source_target_pairs={{1,2},{2,1},{3,4},{4,3},{5,6},{6,5},{7,8},{8,7},{9,10},{10,9},{11,... | collective-permute-start | bytes 122888 | tf_op jit(solution)/shard_map/ppermute | solution.py:296
  39.7 4.7 %all-gather.5 = f32[160,128]{1,0:T(8,128)S(1)} all-gather(f32[80,128]{1,0:T(8,128)S(1)} %get-tuple-element.41), channel_id=7, replica_groups={{0,1},{2,3},{4,5},{6,7},{8,9},{10,11},{12,13},{14,15},{16,17},{18,19},{..., dimensions={0}, use_global_device_ids=true | all-gather | bytes 122880 | tf_op jit(solution)/shard_map/all_gather | solution.py:297
  44.4 0.0 collective-permute-done.1.odd_tile
  44.4 1.0 %shard_map.95 = f32[2,64,128]{2,1,0:T(8,128)} custom-call(f32[2,80,128]{2,1,0:T(8,128)S(1)} %bitcast.30, f32[80,128]{1,0:T(8,128)S(1)} %collective-permute-done.1.odd_tile, f32[8,512]{1,0:T(8,128)S(1)} %get-tuple-element.43.mid, f32[16,512]{1,0:T(8,128)S(1)} %get-tuple-element.34.own, s32[16,512]{1,0:T(8,128)S(1)} %get-tuple-element.35.ids, ...), custom_call_target="tpu_custom_call" | custom-call | tf_op jit(solution)/shard_map/pallas_call | solution.py:272
  (2 shorter events, 0.1 us)
Async XLA Ops:
  11.1 12.7 %collective-permute-start = (f32[120,128]{1,0:T(8,128)S(1)}, f32[120,128]{1,0:T(8,128)S(1)}, u32[]{:S(2)}, u32[]{:S(2)}) collective-permute-start(f32[120,128]{1,0:T(8,128)S(1)} %get-tuple-element.32), channel_id=1, source_target_pairs={{1,2},{2,1},{3,4},{4,3},{5,6},{6,5},{7,8},{8,7},{9,10},{10,9},{11,... | collective-permute-start | bytes 184328 | tf_op jit(solution)/shard_map/ppermute | solution.py:296
  34.3 10.1 %collective-permute-start.1 = (f32[80,128]{1,0:T(8,128)S(1)}, f32[80,128]{1,0:T(8,128)S(1)}, u32[]{:S(2)}, u32[]{:S(2)}) collective-permute-start(f32[80,128]{1,0:T(8,128)S(1)} %get-tuple-element.42), channel_id=1, source_target_pairs={{1,2},{2,1},{3,4},{4,3},{5,6},{6,5},{7,8},{8,7},{9,10},{10,9},{11,... | collective-permute-start | bytes 122888 | tf_op jit(solution)/shard_map/ppermute | solution.py:296

commit v7 on v5

--- a/solution.py
+++ b/solution.py
@@ -34,9 +34,8 @@
 
 
 def gather(fields, lane_hot, block_mask):
-    high, low = halves(jnp.concatenate(fields, axis=0))
-    table = jnp.concatenate([high, low], axis=1)
-    picked = jnp.dot(table, jnp.concatenate([lane_hot, lane_hot], axis=0), preferred_element_type=F32)
+    table = jnp.concatenate(fields, axis=0).astype(BF16)
+    picked = jnp.dot(table, lane_hot, preferred_element_type=F32)
     blocks = block_mask.shape[0]
     return [
         jnp.sum(jnp.where(block_mask, picked[i * blocks : (i + 1) * blocks], 0.0), axis=0, keepdims=True)

time: 45.7 us -> 45.6 us (level)
  no operation moved by 1% of the time
where the time goes in v7:
time: 45.6 us; the launch traced here: 45.4 us
  blocking collectives  28.7 us (63%)
  starting transfers between devices  13.2 us (29%)
  Pallas kernels  3.41 us (7%)
    all_gather x2, blocking collectives, trade_secs(): return (even_in, lax.all_gather(odd, axes, axis_index_groups=sec_odd))  15.5 us
    ppermute x2, starting transfers between devices, trade_tiles(): lax.ppermute(odd, axes, [q for a, b in tile_odd for q in ((a, b), (b, a))])  13.2 us
    all_gather x2, blocking collectives, trade_tiles(): return (lax.all_gather(even, axes, axis_index_groups=tile_even), swapped)  9.58 us
    all_gather x2, blocking collectives, trade_secs(): even_in = lax.all_gather(even, axes, axis_index_groups=sec_even)  3.66 us
    pallas_call x5, Pallas kernels, call(): pl.pallas_call(kernel, out_shape=[jax.ShapeDtypeStruct(s, d) for s, d in...  3.41 us
  transfers between devices with their start and end apart: 2, of which 0 were waited for; matrix products, arithmetic and copies ran while one was open for 0% of the time, Pallas kernels for 0%

profile of v7, /device:TPU:320, one launch (start us, length us, event | category | flops | bytes accessed | tf_op | source)
XLA Modules:
  0.0 45.4 jit_solution(8578012062093101598)
XLA Ops:
  0.0 1.4 %shard_map.91 = (f32[40,128]{1,0:T(8,128)S(1)}, f32[40,128]{1,0:T(8,128)S(1)}, f32[16,512]{1,0:T(8,128)S(1)}, s32[16,512]{1,0:T(8,128)S(1)}, f32[2,64,128]{2,1,0:T(8,128)S(1)}, /*index=5*/f32[64,128]{1,0:T(8,128)S(1)}) custom-call(s32[1,3]{1,0:T(1,128)} %r_0_.1, f32[2,64,128]{2,1,0:T(8,128)} %bitcast.35, f32[64,128]{1,0:T(8,128)} %bitcast.36, ...), custom_call_target="tpu_custom_call" | custom-call | tf_op jit(solution)/shard_map/pallas_call | solution.py:257
  1.4 1.8 %all-gather = f32[80,128]{1,0:T(8,128)S(1)} all-gather(f32[40,128]{1,0:T(8,128)S(1)} %get-tuple-element.26), channel_id=2, replica_groups={{0,64},{1,65},{2,66},{3,67},{4,68},{5,69},{6,70},{7,71},{8,72},{9,73},{..., dimensions={0}, use_global_device_ids=true | all-gather | bytes 61440 | tf_op jit(solution)/shard_map/all_gather | solution.py:285
  3.3 7.8 %all-gather.1 = f32[80,128]{1,0:T(8,128)S(1)} all-gather(f32[40,128]{1,0:T(8,128)S(1)} %get-tuple-element.28), channel_id=3, replica_groups={{64,128},{65,129},{66,130},{67,131},{68,132},{69,133},{70,134},{71,135}..., dimensions={0}, use_global_device_ids=true | all-gather | bytes 61440 | tf_op jit(solution)/shard_map/all_gather | solution.py:287
  11.1 7.8 %collective-permute-start = (f32[120,128]{1,0:T(8,128)S(1)}, f32[120,128]{1,0:T(8,128)S(1)}, u32[]{:S(2)}, u32[]{:S(2)}) collective-permute-start(f32[120,128]{1,0:T(8,128)S(1)} %get-tuple-element.32), channel_id=1, source_target_pairs={{1,2},{2,1},{3,4},{4,3},{5,6},{6,5},{7,8},{8,7},{9,10},{10,9},{11,... | collective-permute-start | bytes 184328 | tf_op jit(solution)/shard_map/ppermute | solution.py:281
  18.8 4.9 %all-gather.2 = f32[240,128]{1,0:T(8,128)S(1)} all-gather(f32[120,128]{1,0:T(8,128)S(1)} %get-tuple-element.31), channel_id=4, replica_groups={{0,1},{2,3},{4,5},{6,7},{8,9},{10,11},{12,13},{14,15},{16,17},{18,19},{..., dimensions={0}, use_global_device_ids=true | all-gather | bytes 184320 | tf_op jit(solution)/shard_map/all_gather | solution.py:282
  23.7 0.0 collective-permute-done.odd_tile
  23.7 0.9 %shard_map.93 = (f32[2,64,128]{2,1,0:T(8,128)S(1)}, f32[64,128]{1,0:T(8,128)S(1)}, f32[24,128]{1,0:T(8,128)S(1)}, f32[24,128]{1,0:T(8,128)S(1)}) custom-call(f32[2,120,128]{2,1,0:T(8,128)S(1)} %bitcast.29, f32[120,128]{1,0:T(8,128)S(1)} %collective-permute-done.odd_tile, f32[8,512]{1,0:T(8,128)S(1)} %get-tuple-element.33.mid, ...), custom_call_target="tpu_custom_call" | custom-call | tf_op jit(solution)/shard_map/pallas_call | solution.py:257
  24.6 1.8 %all-gather.3 = f32[48,128]{1,0:T(8,128)S(1)} all-gather(f32[24,128]{1,0:T(8,128)S(1)} %get-tuple-element.37), channel_id=5, replica_groups={{0,64},{1,65},{2,66},{3,67},{4,68},{5,69},{6,70},{7,71},{8,72},{9,73},{..., dimensions={0}, use_global_device_ids=true | all-gather | bytes 36864 | tf_op jit(solution)/shard_map/all_gather | solution.py:285
  26.5 7.7 %all-gather.4 = f32[48,128]{1,0:T(8,128)S(1)} all-gather(f32[24,128]{1,0:T(8,128)S(1)} %get-tuple-element.39), channel_id=6, replica_groups={{64,128},{65,129},{66,130},{67,131},{68,132},{69,133},{70,134},{71,135}..., dimensions={0}, use_global_device_ids=true | all-gather | bytes 36864 | tf_op jit(solution)/shard_map/all_gather | solution.py:287
  34.2 5.4 %collective-permute-start.1 = (f32[80,128]{1,0:T(8,128)S(1)}, f32[80,128]{1,0:T(8,128)S(1)}, u32[]{:S(2)}, u32[]{:S(2)}) collective-permute-start(f32[80,128]{1,0:T(8,128)S(1)} %get-tuple-element.42), channel_id=1, source_target_pairs={{1,2},{2,1},{3,4},{4,3},{5,6},{6,5},{7,8},{8,7},{9,10},{10,9},{11,... | collective-permute-start | bytes 122888 | tf_op jit(solution)/shard_map/ppermute | solution.py:281
  39.7 4.7 %all-gather.5 = f32[160,128]{1,0:T(8,128)S(1)} all-gather(f32[80,128]{1,0:T(8,128)S(1)} %get-tuple-element.41), channel_id=7, replica_groups={{0,1},{2,3},{4,5},{6,7},{8,9},{10,11},{12,13},{14,15},{16,17},{18,19},{..., dimensions={0}, use_global_device_ids=true | all-gather | bytes 122880 | tf_op jit(solution)/shard_map/all_gather | solution.py:282
  44.3 0.0 collective-permute-done.1.odd_tile
  44.4 1.0 %shard_map.95 = f32[2,64,128]{2,1,0:T(8,128)} custom-call(f32[2,80,128]{2,1,0:T(8,128)S(1)} %bitcast.30, f32[80,128]{1,0:T(8,128)S(1)} %collective-permute-done.1.odd_tile, f32[8,512]{1,0:T(8,128)S(1)} %get-tuple-element.43.mid, f32[16,512]{1,0:T(8,128)S(1)} %get-tuple-element.34.own, s32[16,512]{1,0:T(8,128)S(1)} %get-tuple-element.35.ids, ...), custom_call_target="tpu_custom_call" | custom-call | tf_op jit(solution)/shard_map/pallas_call | solution.py:257
  (2 shorter events, 0.1 us)
Async XLA Ops:
  11.1 12.7 %collective-permute-start = (f32[120,128]{1,0:T(8,128)S(1)}, f32[120,128]{1,0:T(8,128)S(1)}, u32[]{:S(2)}, u32[]{:S(2)}) collective-permute-start(f32[120,128]{1,0:T(8,128)S(1)} %get-tuple-element.32), channel_id=1, source_target_pairs={{1,2},{2,1},{3,4},{4,3},{5,6},{6,5},{7,8},{8,7},{9,10},{10,9},{11,... | collective-permute-start | bytes 184328 | tf_op jit(solution)/shard_map/ppermute | solution.py:281
  34.2 10.1 %collective-permute-start.1 = (f32[80,128]{1,0:T(8,128)S(1)}, f32[80,128]{1,0:T(8,128)S(1)}, u32[]{:S(2)}, u32[]{:S(2)}) collective-permute-start(f32[80,128]{1,0:T(8,128)S(1)} %get-tuple-element.42), channel_id=1, source_target_pairs={{1,2},{2,1},{3,4},{4,3},{5,6},{6,5},{7,8},{8,7},{9,10},{10,9},{11,... | collective-permute-start | bytes 122888 | tf_op jit(solution)/shard_map/ppermute | solution.py:281
